TPU v7x, 512 devices: a whole 4x8x8 slice. The times are simulated.
512 devices in a mesh: lat: 16 (over x_lo, y), lon: 32 (over x_hi, z, core).
Axes of the slice: x: 4 (x_hi: 2, x_lo: 2; x = x_hi * 2 + x_lo), y: 8, z: 8, core: 2. Of those that a mesh axis runs over, the one named last changes fastest.
Arguments:
- tokens: bfloat16 [2, 192, 768, 192], P(None, 'lat', 'lon'), may hold values from -6 to 6
- norm_gain: float32 [192], replicated, may hold values from 0.1 to 1.9
- qkv_weight: bfloat16 [192, 576], replicated, may hold values from -0.4375 to 0.4375
- proj_weight: bfloat16 [192, 192], replicated, may hold values from -0.4375 to 0.4375
- merge_gain: float32 [768], replicated, may hold values from 0.1 to 1.9
- merge_weight: bfloat16 [768, 384], replicated, may hold values from -0.21875 to 0.21875
- coarse_gain: float32 [384], replicated, may hold values from 0.1 to 1.9
- coarse_qkv: bfloat16 [384, 1152], replicated, may hold values from -0.3125 to 0.3125
- coarse_proj: bfloat16 [384, 384], replicated, may hold values from -0.3125 to 0.3125
- up_weight: bfloat16 [384, 768], replicated, may hold values from -0.3125 to 0.3125
- up_gain: float32 [192], replicated, may hold values from 0.1 to 1.9
- out_weight: bfloat16 [192, 192], replicated, may hold values from -0.4375 to 0.4375
Outputs:
- encoded: bfloat16 [2, 192, 768, 192], P(None, 'lat', 'lon')
All inputs are finite; a program needn't handle non-finite values.
Results may differ from a plain program's by a relative error of at most 0.02.
Values may be sent and summed in bfloat16 or wider, within the bound.
A program may use at most 64 MiB of HBM per device.

v0:
```python
import jax
import jax.numpy as jnp
from jax import lax
from jax.sharding import PartitionSpec as P

FINE_HEADS = 6
COARSE_HEADS = 12
WIN_LAT = 6
WIN_LON = 12


EPSILON = 1e-05


def extended_2(cells, sides, width, closed):
    for axis, dim in sides:
        count = lax.axis_size(axis)
        ends = count if closed else count - 1
        head = lax.slice_in_dim(cells, 0, width, axis=dim)
        tail = lax.slice_in_dim(cells, cells.shape[dim] - width, cells.shape[dim], axis=dim)
        cells = jnp.concatenate(
            [
                lax.ppermute(tail, axis, [(i, (i + 1) % count) for i in range(ends)]),
                cells,
                lax.ppermute(head, axis, [((i + 1) % count, i) for i in range(ends)]),
            ],
            axis=dim,
        )
    return cells


def layer_norm(values, norm_gain):
    average = jnp.mean(values, axis=-1, keepdims=True)
    centred = values - average
    spread = jnp.mean(centred * centred, axis=-1, keepdims=True)
    return (centred * lax.rsqrt(spread + EPSILON) * norm_gain).astype(jnp.bfloat16)


def window_heads(stripe, norm_gain, qkv_weight, head_count, lat_pair):
    levels, row_count, col_count, channels = stripe.shape
    head_dim = channels // head_count
    normed = layer_norm(stripe.astype(jnp.float32), norm_gain)
    packed = jnp.dot(
        normed.reshape(-1, channels), qkv_weight, preferred_element_type=jnp.float32
    ).astype(jnp.bfloat16)
    packed = packed.reshape(
        levels // 2, 2, row_count, col_count // WIN_LON, WIN_LON, 3, head_count, head_dim
    )
    packed = packed.transpose(0, 3, 5, 6, 1, 2, 4, 7)
    window_len = 2 * row_count * WIN_LON
    packed = packed.reshape(levels // 2, col_count // WIN_LON, 3, head_count, window_len, head_dim)
    scores = jnp.einsum(
        "abhtd,abhsd->abhts", packed[:, :, 0], packed[:, :, 1], preferred_element_type=jnp.float32
    )
    scores = scores * head_dim ** (-0.5)
    level_ids = jnp.arange(levels // 2)
    diagonal = jnp.eye(2, dtype=jnp.bool_)
    level_mask = (level_ids[:, None, None] != levels // 2 - 1) | diagonal[None]
    allowed = (
        level_mask[:, :, None, None, :, None, None] & lat_pair[None, None, :, None, None, :, None]
    )
    allowed = jnp.broadcast_to(allowed, (levels // 2, 2, row_count, WIN_LON, 2, row_count, WIN_LON))
    allowed = allowed.reshape(levels // 2, window_len, window_len)
    raised = jnp.where(allowed[:, None, None], jnp.exp(scores), 0.0)
    weights = (raised / jnp.sum(raised, axis=-1, keepdims=True)).astype(jnp.bfloat16)
    attended = jnp.einsum(
        "abhts,abhsd->abhtd", weights, packed[:, :, 2], preferred_element_type=jnp.float32
    ).astype(jnp.bfloat16)
    attended = attended.reshape(
        levels // 2, col_count // WIN_LON, head_count, 2, row_count, WIN_LON, head_dim
    )
    attended = attended.transpose(0, 3, 4, 1, 5, 2, 6).reshape(
        levels, row_count, col_count, channels
    )
    return attended


def block_heads(extended, first_row, lat_total, norm_gain, qkv_weight, head_count):
    levels, ext_rows, ext_cols, channels = extended.shape
    rolled = jnp.roll(extended, -1, axis=0)
    strips = ext_rows // WIN_LAT
    grouped = rolled.reshape(levels, strips, WIN_LAT, ext_cols, channels).transpose(1, 0, 2, 3, 4)
    row_ids = first_row + jnp.arange(ext_rows, dtype=jnp.int32).reshape(strips, WIN_LAT)
    row_valid = (row_ids >= 0) & (row_ids < lat_total)
    lat_pairs = jnp.broadcast_to(row_valid[:, None, :], (strips, WIN_LAT, WIN_LAT))

    def one_strip(packet):
        return window_heads(packet[0], norm_gain, qkv_weight, head_count, packet[1])

    attended = lax.map(one_strip, (grouped, lat_pairs))
    attended = attended.transpose(1, 0, 2, 3, 4).reshape(levels, ext_rows, ext_cols, channels)
    return jnp.roll(attended, 1, axis=0)


def project_add(base_part, attended, proj_weight):
    branch = jnp.dot(
        attended.reshape(-1, attended.shape[-1]), proj_weight, preferred_element_type=jnp.float32
    )
    return (base_part.astype(jnp.float32) + branch.reshape(base_part.shape)).astype(jnp.bfloat16)


def merge_patches(fine_out, merge_gain, merge_weight):
    levels, lat_count, lon_count, channels = fine_out.shape
    stacked = fine_out.reshape(levels, lat_count // 2, 2, lon_count // 2, 2, channels)
    stacked = stacked.transpose(0, 1, 3, 4, 2, 5).reshape(
        levels, lat_count // 2, lon_count // 2, 4 * channels
    )
    normed = layer_norm(stacked.astype(jnp.float32), merge_gain)
    merged = jnp.dot(
        normed.reshape(-1, 4 * channels), merge_weight, preferred_element_type=jnp.float32
    )
    return merged.astype(jnp.bfloat16).reshape(
        levels, lat_count // 2, lon_count // 2, merge_weight.shape[1]
    )


def expand(coarse_out, fine_out, up_weight, up_gain, out_weight):
    levels, lat_count, lon_count, coarse_width = coarse_out.shape
    channels = fine_out.shape[-1]
    lifted = jnp.dot(
        coarse_out.reshape(-1, coarse_width), up_weight, preferred_element_type=jnp.float32
    )
    lifted = lifted.reshape(levels, lat_count, lon_count, 2, 2, channels)
    lifted = lifted.transpose(0, 1, 4, 2, 3, 5).reshape(
        levels, 2 * lat_count, 2 * lon_count, channels
    )
    normed = layer_norm(lifted, up_gain)
    branch = jnp.dot(normed.reshape(-1, channels), out_weight, preferred_element_type=jnp.float32)
    return (fine_out.astype(jnp.float32) + branch.reshape(fine_out.shape)).astype(jnp.bfloat16)


def body(
    tokens,
    norm_gain,
    qkv_weight,
    proj_weight,
    merge_gain,
    merge_weight,
    coarse_gain,
    coarse_qkv,
    coarse_proj,
    up_weight,
    up_gain,
    out_weight,
):
    levels, row_count, col_count, channels = tokens.shape
    half_lat = WIN_LAT // 2
    half_lon = WIN_LON // 2
    lat_index = lax.axis_index("lat")
    lat_devices = lax.axis_size("lat")
    row_wide = extended_2(tokens, (("lat", 1),), half_lat, False)
    extended = extended_2(row_wide, (("lon", 2),), half_lon, True)
    attended = block_heads(
        extended,
        lat_index * row_count - half_lat,
        lat_devices * row_count,
        norm_gain,
        qkv_weight,
        FINE_HEADS,
    )
    own_part = attended[:, half_lat : half_lat + row_count, half_lon : half_lon + col_count]
    fine_out = project_add(tokens, own_part, proj_weight)
    coarse_rows = row_count // 2
    coarse_cols = col_count // 2
    coarse = merge_patches(fine_out, merge_gain, merge_weight)
    coarse_tall = extended_2(coarse, (("lat", 1),), half_lat, False)
    coarse_wide = extended_2(coarse_tall, (("lon", 2),), half_lon, True)
    coarse_att = block_heads(
        coarse_wide,
        lat_index * coarse_rows - half_lat,
        lat_devices * coarse_rows,
        coarse_gain,
        coarse_qkv,
        COARSE_HEADS,
    )
    coarse_own = coarse_att[:, half_lat : half_lat + coarse_rows, half_lon : half_lon + coarse_cols]
    coarse_out = project_add(coarse, coarse_own, coarse_proj)
    return expand(coarse_out, fine_out, up_weight, up_gain, out_weight)


def solution(mesh):
    placed = (P(None, "lat", "lon", None), P(), P(), P(), P(), P(), P(), P(), P(), P(), P(), P())
    return jax.shard_map(
        body, mesh=mesh, in_specs=placed, out_specs=P(None, "lat", "lon", None), check_vma=False
    )
```

profile of v0, /device:TPU:24, one launch (start us, length us, event | category | flops | bytes accessed | tf_op | source)
XLA Modules:
  0.0 174.9 jit_solution(7283019634290639363)
XLA Ops:
  0.0 1.0 fusion.58
  1.0 4.7 %collective-permute-start = (bf16[2,3,24,192]{3,2,1,0:T(8,128)(2,1)S(1)}, bf16[2,3,24,192]{3,2,1,0:T(8,128)(2,1)S(1)}, u32[]{:S(2)}, u32[]{:S(2)}) collective-permute-start(bf16[2,3,24,192]{3,2,1,0:T(8,128)(2,1)S(1)} %get-tuple-element.151), channel_id=1, source_target_pairs={{0,32},{32,64},{64,96},{96,128},{128,160},{160,192},{192,224},{224... | collective-permute-start | bytes 165896 | tf_op jit(solution)/shard_map/ppermute | solution.py:23
  5.7 1.9 %collective-permute-start.1 = (bf16[2,3,24,192]{3,2,1,0:T(8,128)(2,1)S(1)}, bf16[2,3,24,192]{3,2,1,0:T(8,128)(2,1)S(1)}, u32[]{:S(2)}, u32[]{:S(2)}) collective-permute-start(bf16[2,3,24,192]{3,2,1,0:T(8,128)(2,1)S(1)} %get-tuple-element.150), channel_id=1, source_target_pairs={{32,0},{64,32},{96,64},{128,96},{160,128},{192,160},{224,192},{256... | collective-permute-start | bytes 165896 | tf_op jit(solution)/shard_map/ppermute | solution.py:25
  7.7 1.0 constant_dynamic-update-slice_fusion.3
  8.7 4.5 %collective-permute-done.1 = bf16[2,3,24,192]{3,2,1,0:T(8,128)(2,1)S(1)} collective-permute-done((bf16[2,3,24,192]{3,2,1,0:T(8,128)(2,1)S(1)}, bf16[2,3,24,192]{3,2,1,0:T(8,128)(2,1)S(1)}, u32[]{:S(2)}, u32[]{:S(2)}) %collective-permute-start.1) | collective-permute-done | bytes 55328 | tf_op jit(solution)/shard_map/ppermute | solution.py:25
  13.2 1.9 %collective-permute-start.2 = (bf16[2,18,6,192]{3,2,1,0:T(8,128)(2,1)S(1)}, bf16[2,18,6,192]{3,2,1,0:T(8,128)(2,1)S(1)}, u32[]{:S(2)}, u32[]{:S(2)}) collective-permute-start(bf16[2,18,6,192]{3,2,1,0:T(8,128)(2,1)S(1)} %get-tuple-element.146), channel_id=1, source_target_pairs={{0,1},{1,2},{2,3},{3,4},{4,5},{5,6},{6,7},{7,8},{8,9},{9,10},{10,1... | collective-permute-start | bytes 248840 | tf_op jit(solution)/shard_map/ppermute | solution.py:23
  15.1 11.4 %collective-permute-start.3 = (bf16[2,18,6,192]{3,2,1,0:T(8,128)(2,1)S(1)}, bf16[2,18,6,192]{3,2,1,0:T(8,128)(2,1)S(1)}, u32[]{:S(2)}, u32[]{:S(2)}) collective-permute-start(bf16[2,18,6,192]{3,2,1,0:T(8,128)(2,1)S(1)} %get-tuple-element.147), channel_id=1, source_target_pairs={{1,0},{2,1},{3,2},{4,3},{5,4},{6,5},{7,6},{8,7},{9,8},{10,9},{11,1... | collective-permute-start | bytes 248840 | tf_op jit(solution)/shard_map/ppermute | solution.py:25
  26.6 0.8 collective-permute-done.2
  27.5 1.8 %collective-permute-done.3 = bf16[2,18,6,192]{3,2,1,0:T(8,128)(2,1)S(1)} collective-permute-done((bf16[2,18,6,192]{3,2,1,0:T(8,128)(2,1)S(1)}, bf16[2,18,6,192]{3,2,1,0:T(8,128)(2,1)S(1)}, u32[]{:S(2)}, u32[]{:S(2)}) %collective-permute-start.3) | collective-permute-done | bytes 82976 | tf_op jit(solution)/shard_map/ppermute | solution.py:25
  29.8 1.4 copy.91
  31.2 51.0 %while.20 = (s32[]{:T(128)}, bf16[3,2,6,36,192]{4,1,3,2,0:T(2,128)(2,1)}, pred[3,6,6]{2,1,0:T(8,128)(4,1)S(1)}, bf16[3,2,6,36,192]{4,1,3,2,0:T(2,128)(2,1)}, f32...) while((s32[]{:T(128)}, bf16[3,2,6,36,192]{4,1,3,2,0:T(2,128)(2,1)}, ...), condition=%wide.region_4.5_spmd, body=%wide.region_0.4_spmd.sunk | while | flops 147182112 | bytes 14074481 | solution.py:90
  31.2 1.1 constant_dynamic-slice_fusion.2
  33.0 1.2 convolution_convert_fusion.5
  34.2 3.2 %reshape.393 = bf16[1,2,6,3,12,3,6,32]{7,6,5,4,3,2,1,0:T(8,128)(2,1)S(1)} reshape(bf16[432,576]{1,0:T(8,128)(2,1)} %convolution_convert_fusion.5) | data formatting | bytes 995328 | tf_op jit(solution)/shard_map/while/body/eval_jaxpr/reshape | solution.py:46
  37.5 2.2 %copy.155 = bf16[1,3,3,6,2,6,12,32]{7,6,5,4,3,2,1,0:T(8,128)(2,1)} copy(bf16[1,3,3,6,2,6,12,32]{7,3,2,6,1,5,4,0:T(8,128)(2,1)S(1)} %bitcast.185) | data formatting | bytes 995328 | tf_op jit(solution)/shard_map/while/body/eval_jaxpr/transpose | solution.py:49
  39.7 3.6 %reshape.394 = bf16[1,3,3,6,144,32]{5,4,3,2,1,0:T(8,128)(2,1)S(1)} reshape(bf16[1,3,3,6,2,6,12,32]{7,6,5,4,3,2,1,0:T(8,128)(2,1)} %copy.155) | data formatting | bytes 995328 | tf_op jit(solution)/shard_map/while/body/eval_jaxpr/reshape | solution.py:51
  47.4 0.8 constant_dynamic-update-slice_fusion.10
  48.2 1.1 constant_dynamic-slice_fusion.2
  50.0 1.2 convolution_convert_fusion.5
  51.2 3.2 %reshape.393 = bf16[1,2,6,3,12,3,6,32]{7,6,5,4,3,2,1,0:T(8,128)(2,1)S(1)} reshape(bf16[432,576]{1,0:T(8,128)(2,1)} %convolution_convert_fusion.5) | data formatting | bytes 995328 | tf_op jit(solution)/shard_map/while/body/eval_jaxpr/reshape | solution.py:46
  54.5 2.2 %copy.155 = bf16[1,3,3,6,2,6,12,32]{7,6,5,4,3,2,1,0:T(8,128)(2,1)} copy(bf16[1,3,3,6,2,6,12,32]{7,3,2,6,1,5,4,0:T(8,128)(2,1)S(1)} %bitcast.185) | data formatting | bytes 995328 | tf_op jit(solution)/shard_map/while/body/eval_jaxpr/transpose | solution.py:49
  56.7 3.6 %reshape.394 = bf16[1,3,3,6,144,32]{5,4,3,2,1,0:T(8,128)(2,1)S(1)} reshape(bf16[1,3,3,6,2,6,12,32]{7,6,5,4,3,2,1,0:T(8,128)(2,1)} %copy.155) | data formatting | bytes 995328 | tf_op jit(solution)/shard_map/while/body/eval_jaxpr/reshape | solution.py:51
  64.4 0.8 constant_dynamic-update-slice_fusion.10
  65.2 1.1 constant_dynamic-slice_fusion.2
  67.0 1.2 convolution_convert_fusion.5
  68.2 3.2 %reshape.393 = bf16[1,2,6,3,12,3,6,32]{7,6,5,4,3,2,1,0:T(8,128)(2,1)S(1)} reshape(bf16[432,576]{1,0:T(8,128)(2,1)} %convolution_convert_fusion.5) | data formatting | bytes 995328 | tf_op jit(solution)/shard_map/while/body/eval_jaxpr/reshape | solution.py:46
  71.5 2.2 %copy.155 = bf16[1,3,3,6,2,6,12,32]{7,6,5,4,3,2,1,0:T(8,128)(2,1)} copy(bf16[1,3,3,6,2,6,12,32]{7,3,2,6,1,5,4,0:T(8,128)(2,1)S(1)} %bitcast.185) | data formatting | bytes 995328 | tf_op jit(solution)/shard_map/while/body/eval_jaxpr/transpose | solution.py:49
  73.7 3.6 %reshape.394 = bf16[1,3,3,6,144,32]{5,4,3,2,1,0:T(8,128)(2,1)S(1)} reshape(bf16[1,3,3,6,2,6,12,32]{7,6,5,4,3,2,1,0:T(8,128)(2,1)} %copy.155) | data formatting | bytes 995328 | tf_op jit(solution)/shard_map/while/body/eval_jaxpr/reshape | solution.py:51
  81.4 0.9 constant_dynamic-update-slice_fusion.10
  82.2 1.2 copy.135
  86.9 1.9 %collective-permute-start.4 = (bf16[2,3,12,384]{3,2,1,0:T(8,128)(2,1)S(1)}, bf16[2,3,12,384]{3,2,1,0:T(8,128)(2,1)S(1)}, u32[]{:S(2)}, u32[]{:S(2)}) collective-permute-start(bf16[2,3,12,384]{3,2,1,0:T(8,128)(2,1)S(1)} %get-tuple-element.153), channel_id=1, source_target_pairs={{0,32},{32,64},{64,96},{96,128},{128,160},{160,192},{192,224},{224... | collective-permute-start | bytes 165896 | tf_op jit(solution)/shard_map/ppermute | solution.py:23
  88.9 1.1 copy.96
  89.9 3.9 %collective-permute-start.5 = (bf16[2,3,12,384]{3,2,1,0:T(8,128)(2,1)S(1)}, bf16[2,3,12,384]{3,2,1,0:T(8,128)(2,1)S(1)}, u32[]{:S(2)}, u32[]{:S(2)}) collective-permute-start(bf16[2,3,12,384]{3,2,1,0:T(8,128)(2,1)S(1)} %get-tuple-element.152), channel_id=1, source_target_pairs={{32,0},{64,32},{96,64},{128,96},{160,128},{192,160},{224,192},{256... | collective-permute-start | bytes 165896 | tf_op jit(solution)/shard_map/ppermute | solution.py:25
  93.9 3.5 %collective-permute-done.5 = bf16[2,3,12,384]{3,2,1,0:T(8,128)(2,1)S(1)} collective-permute-done((bf16[2,3,12,384]{3,2,1,0:T(8,128)(2,1)S(1)}, bf16[2,3,12,384]{3,2,1,0:T(8,128)(2,1)S(1)}, u32[]{:S(2)}, u32[]{:S(2)}) %collective-permute-start.5) | collective-permute-done | bytes 55328 | tf_op jit(solution)/shard_map/ppermute | solution.py:25
  97.4 1.9 %collective-permute-start.6 = (bf16[2,12,6,384]{3,2,1,0:T(8,128)(2,1)S(1)}, bf16[2,12,6,384]{3,2,1,0:T(8,128)(2,1)S(1)}, u32[]{:S(2)}, u32[]{:S(2)}) collective-permute-start(bf16[2,12,6,384]{3,2,1,0:T(8,128)(2,1)S(1)} %get-tuple-element.148), channel_id=1, source_target_pairs={{0,1},{1,2},{2,3},{3,4},{4,5},{5,6},{6,7},{7,8},{8,9},{9,10},{10,1... | collective-permute-start | bytes 331784 | tf_op jit(solution)/shard_map/ppermute | solution.py:23
  99.4 7.3 %collective-permute-start.7 = (bf16[2,12,6,384]{3,2,1,0:T(8,128)(2,1)S(1)}, bf16[2,12,6,384]{3,2,1,0:T(8,128)(2,1)S(1)}, u32[]{:S(2)}, u32[]{:S(2)}) collective-permute-start(bf16[2,12,6,384]{3,2,1,0:T(8,128)(2,1)S(1)} %get-tuple-element.149), channel_id=1, source_target_pairs={{1,0},{2,1},{3,2},{4,3},{5,4},{6,5},{7,6},{8,7},{9,8},{10,9},{11,1... | collective-permute-start | bytes 331784 | tf_op jit(solution)/shard_map/ppermute | solution.py:25
  106.7 0.9 collective-permute-done.6
  107.5 1.8 %collective-permute-done.7 = bf16[2,12,6,384]{3,2,1,0:T(8,128)(2,1)S(1)} collective-permute-done((bf16[2,12,6,384]{3,2,1,0:T(8,128)(2,1)S(1)}, bf16[2,12,6,384]{3,2,1,0:T(8,128)(2,1)S(1)}, u32[]{:S(2)}, u32[]{:S(2)}) %collective-permute-start.7) | collective-permute-done | bytes 110624 | tf_op jit(solution)/shard_map/ppermute | solution.py:25
  109.6 0.8 pad_maximum_fusion.3
  110.4 58.3 %while.21 = (s32[]{:T(128)}, bf16[2,2,6,24,384]{4,3,2,1,0:T(8,128)(2,1)}, pred[2,6,6]{2,1,0:T(8,128)(4,1)S(1)}, bf16[2,2,6,24,384]{4,3,2,0,1:T(8,128)(2,1)}, f32...) while((s32[]{:T(128)}, bf16[2,2,6,24,384]{4,3,2,1,0:T(8,128)(2,1)}, ...), condition=%wide.region_11.12_spmd, body=%wide.region_7.11_spmd.sunk | while | flops 323644480 | bytes 19170292 | solution.py:90
  110.4 1.1 fusion.90
  111.5 1.1 fusion.91
  112.8 1.0 bitcast_convert_fusion.2
  114.0 1.7 convolution_convert_fusion.6
  115.7 3.9 %reshape.396 = bf16[1,2,6,2,12,3,12,32]{7,6,5,4,3,2,1,0:T(8,128)(2,1)} reshape(bf16[288,1152]{1,0:T(8,128)(2,1)S(1)} %convolution_convert_fusion.6) | data formatting | bytes 1327104 | tf_op jit(solution)/shard_map/while/body/eval_jaxpr/reshape | solution.py:46
  119.5 4.7 %copy.159 = bf16[1,2,3,12,2,6,12,32]{7,1,6,5,4,3,2,0:T(2,128)(2,1)S(1)} copy(bf16[1,2,3,12,2,6,12,32]{7,3,2,6,1,5,4,0:T(8,128)(2,1)} %bitcast.184) | data formatting | bytes 1327104 | tf_op jit(solution)/shard_map/while/body/eval_jaxpr/transpose | solution.py:49
  124.3 1.9 %fusion.93 = (bf16[1,2,1,12,144,32]{5,1,4,3,2,0:T(2,128)(2,1)S(1)}, bf16[1,2,1,12,144,32]{5,1,4,3,2,0:T(2,128)(2,1)S(1)}, bf16[1,2,1,12,144,32]{5,1,4,3,2,0:T(2,128)(2,1)S(1)}) fusion(bf16[1,2,3,12,144,32]{5,1,4,3,2,0:T(2,128)(2,1)S(1)} %bitcast.186), kind=kLoop, calls=%fused_computation.105.clone.1 | loop fusion | bytes 1327104 | tf_op jit(solution)/shard_map/while/body/eval_jaxpr/slice | solution.py:67
  126.2 1.8 %copy.160 = bf16[1,2,1,12,144,32]{4,5,3,1,2,0:T(8,128)(2,1)} copy(bf16[1,2,1,12,144,32]{5,1,4,3,2,0:T(2,128)(2,1)S(1)} %get-tuple-element.239) | data formatting | bytes 442368 | tf_op jit(solution)/shard_map/while
  129.5 3.7 %fusion.94 = (f32[2,12,144]{2,1,0:T(8,128)S(1)}, f32[2,12,144,144]{2,3,1,0:T(8,128)}) fusion(pred[144,144]{0,1:T(8,128)(4,1)S(1)} %broadcast_in_dim.132, bf16[1,2,1,12,144,32]{4,5,3,1,2,0:T(8,128)(2,1)} %copy.160, bf16[1,2,1,12,144,32]{4,5,3,1,2,0:T(8,128)(2,1)S(1)} %copy.161), kind=kOutput, calls=%fused_computation.30.clone.1 | convolution fusion | flops 33340032 | bytes 2467584 | tf_op jit(solution)/shard_map/while/body/eval_jaxpr/abhtd,abhsd->abhts/dot_general | solution.py:52
  133.9 2.9 %fusion.95 = bf16[2,12,144,32]{2,3,1,0:T(8,128)(2,1)S(1)} fusion(f32[2,12,144,144]{2,3,1,0:T(8,128)} %get-tuple-element.241, f32[2,12,144]{2,1,0:T(8,128)S(1)} %get-tuple-element.242, pred[144,144]{0,1:T(8,128)(4,1)S(1)} %broadcast_in_dim.132, bf16[1,2,1,12,144,32]{4,5,3,1,2,0:T(8,128)(2,1)S(1)} %copy.162), kind=kOutput, calls=%fused_computation.33.clone.1 | convolution fusion | flops 33951744 | bytes 2467584 | tf_op jit(solution)/shard_map/while/body/eval_jaxpr/abhts,abhsd->abhtd/dot_general | solution.py:66
  139.6 1.0 fusion.90
  140.6 1.1 fusion.91
  142.0 1.0 bitcast_convert_fusion.2
  143.1 1.7 convolution_convert_fusion.6
  144.8 3.9 %reshape.396 = bf16[1,2,6,2,12,3,12,32]{7,6,5,4,3,2,1,0:T(8,128)(2,1)} reshape(bf16[288,1152]{1,0:T(8,128)(2,1)S(1)} %convolution_convert_fusion.6) | data formatting | bytes 1327104 | tf_op jit(solution)/shard_map/while/body/eval_jaxpr/reshape | solution.py:46
  148.7 4.7 %copy.159 = bf16[1,2,3,12,2,6,12,32]{7,1,6,5,4,3,2,0:T(2,128)(2,1)S(1)} copy(bf16[1,2,3,12,2,6,12,32]{7,3,2,6,1,5,4,0:T(8,128)(2,1)} %bitcast.184) | data formatting | bytes 1327104 | tf_op jit(solution)/shard_map/while/body/eval_jaxpr/transpose | solution.py:49
  153.4 1.9 %fusion.93 = (bf16[1,2,1,12,144,32]{5,1,4,3,2,0:T(2,128)(2,1)S(1)}, bf16[1,2,1,12,144,32]{5,1,4,3,2,0:T(2,128)(2,1)S(1)}, bf16[1,2,1,12,144,32]{5,1,4,3,2,0:T(2,128)(2,1)S(1)}) fusion(bf16[1,2,3,12,144,32]{5,1,4,3,2,0:T(2,128)(2,1)S(1)} %bitcast.186), kind=kLoop, calls=%fused_computation.105.clone.1 | loop fusion | bytes 1327104 | tf_op jit(solution)/shard_map/while/body/eval_jaxpr/slice | solution.py:67
  155.3 1.8 %copy.160 = bf16[1,2,1,12,144,32]{4,5,3,1,2,0:T(8,128)(2,1)} copy(bf16[1,2,1,12,144,32]{5,1,4,3,2,0:T(2,128)(2,1)S(1)} %get-tuple-element.239) | data formatting | bytes 442368 | tf_op jit(solution)/shard_map/while
  158.6 3.7 %fusion.94 = (f32[2,12,144]{2,1,0:T(8,128)S(1)}, f32[2,12,144,144]{2,3,1,0:T(8,128)}) fusion(pred[144,144]{0,1:T(8,128)(4,1)S(1)} %broadcast_in_dim.132, bf16[1,2,1,12,144,32]{4,5,3,1,2,0:T(8,128)(2,1)} %copy.160, bf16[1,2,1,12,144,32]{4,5,3,1,2,0:T(8,128)(2,1)S(1)} %copy.161), kind=kOutput, calls=%fused_computation.30.clone.1 | convolution fusion | flops 33340032 | bytes 2467584 | tf_op jit(solution)/shard_map/while/body/eval_jaxpr/abhtd,abhsd->abhts/dot_general | solution.py:52
  163.0 2.9 %fusion.95 = bf16[2,12,144,32]{2,3,1,0:T(8,128)(2,1)S(1)} fusion(f32[2,12,144,144]{2,3,1,0:T(8,128)} %get-tuple-element.241, f32[2,12,144]{2,1,0:T(8,128)S(1)} %get-tuple-element.242, pred[144,144]{0,1:T(8,128)(4,1)S(1)} %broadcast_in_dim.132, bf16[1,2,1,12,144,32]{4,5,3,1,2,0:T(8,128)(2,1)S(1)} %copy.162), kind=kOutput, calls=%fused_computation.33.clone.1 | convolution fusion | flops 33951744 | bytes 2467584 | tf_op jit(solution)/shard_map/while/body/eval_jaxpr/abhts,abhsd->abhtd/dot_general | solution.py:66
  168.7 1.1 fusion.54
  169.8 1.9 %fusion.60 = (f32[2,6,2,12,2]{3,2,4,1,0:T(2,128)S(1)}, f32[2,6,2,12,2,192]{5,3,2,4,1,0:T(8,128)S(1)}) fusion(bf16[2,2,192,384,1,1]{3,2,1,0,5,4:T(8,128)(2,1)} %bitcast.191, bf16[384,384]{1,0:T(8,128)(2,1)} %param.24, bf16[2,6,12,384]{3,2,1,0:T(8,128)(2,1)S(1)} %reshape.349, bf16[1,12,24,384]{3,2,1,0:T(8,128)(2,1)S(1)} %bitcast.196, ...), kind=kOutput, calls=%fused_computation.114 | convolution fusion | flops 127899072 | bytes 1882368 | tf_op jit(solution)/shard_map/dot_general | solution.py:120
  173.1 0.8 multiply_convert_fusion.2
  173.9 1.0 fusion.29
  (166 shorter events, 30.0 us)
Async XLA Ops:
  0.0 86.5 %copy-start = (bf16[768,384]{1,0:T(8,128)(2,1)S(1)}, bf16[768,384]{1,0:T(8,128)(2,1)}, u32[]{:S(2)}) copy-start(bf16[768,384]{1,0:T(8,128)(2,1)} %param.21) | copy-start | bytes 1769476
  1.0 6.7 %collective-permute-start = (bf16[2,3,24,192]{3,2,1,0:T(8,128)(2,1)S(1)}, bf16[2,3,24,192]{3,2,1,0:T(8,128)(2,1)S(1)}, u32[]{:S(2)}, u32[]{:S(2)}) collective-permute-start(bf16[2,3,24,192]{3,2,1,0:T(8,128)(2,1)S(1)} %get-tuple-element.151), channel_id=1, source_target_pairs={{0,32},{32,64},{64,96},{96,128},{128,160},{160,192},{192,224},{224... | collective-permute-start | bytes 165896 | tf_op jit(solution)/shard_map/ppermute | solution.py:23
  5.7 7.5 %collective-permute-start.1 = (bf16[2,3,24,192]{3,2,1,0:T(8,128)(2,1)S(1)}, bf16[2,3,24,192]{3,2,1,0:T(8,128)(2,1)S(1)}, u32[]{:S(2)}, u32[]{:S(2)}) collective-permute-start(bf16[2,3,24,192]{3,2,1,0:T(8,128)(2,1)S(1)} %get-tuple-element.150), channel_id=1, source_target_pairs={{32,0},{64,32},{96,64},{128,96},{160,128},{192,160},{224,192},{256... | collective-permute-start | bytes 165896 | tf_op jit(solution)/shard_map/ppermute | solution.py:25
  13.2 14.3 %collective-permute-start.2 = (bf16[2,18,6,192]{3,2,1,0:T(8,128)(2,1)S(1)}, bf16[2,18,6,192]{3,2,1,0:T(8,128)(2,1)S(1)}, u32[]{:S(2)}, u32[]{:S(2)}) collective-permute-start(bf16[2,18,6,192]{3,2,1,0:T(8,128)(2,1)S(1)} %get-tuple-element.146), channel_id=1, source_target_pairs={{0,1},{1,2},{2,3},{3,4},{4,5},{5,6},{6,7},{7,8},{8,9},{9,10},{10,1... | collective-permute-start | bytes 248840 | tf_op jit(solution)/shard_map/ppermute | solution.py:23
  15.1 14.1 %collective-permute-start.3 = (bf16[2,18,6,192]{3,2,1,0:T(8,128)(2,1)S(1)}, bf16[2,18,6,192]{3,2,1,0:T(8,128)(2,1)S(1)}, u32[]{:S(2)}, u32[]{:S(2)}) collective-permute-start(bf16[2,18,6,192]{3,2,1,0:T(8,128)(2,1)S(1)} %get-tuple-element.147), channel_id=1, source_target_pairs={{1,0},{2,1},{3,2},{4,3},{5,4},{6,5},{7,6},{8,7},{9,8},{10,9},{11,1... | collective-permute-start | bytes 248840 | tf_op jit(solution)/shard_map/ppermute | solution.py:25
  26.6 4.6 %copy-start.1 = (bf16[192,576]{1,0:T(8,128)(2,1)S(1)}, bf16[192,576]{1,0:T(8,128)(2,1)}, u32[]{:S(2)}) copy-start(bf16[192,576]{1,0:T(8,128)(2,1)} %param.18) | copy-start | bytes 663556
  26.6 4.6 %copy-start.11 = (f32[192]{0:T(256)S(1)}, f32[192]{0:T(256)}, u32[]{:S(2)}) copy-start(f32[192]{0:T(256)} %param.17) | copy-start | bytes 2308
  82.2 1.3 copy-start.4
  82.2 1.3 copy-start.9
  83.8 3.0 %copy-start.2 = (f32[2,12,24,192]{3,2,1,0:T(8,128)}, f32[2,12,24,192]{3,2,1,0:T(8,128)S(1)}, u32[]{:S(2)}) copy-start(f32[2,12,24,192]{3,2,1,0:T(8,128)S(1)} %fusion.28) | copy-start | bytes 1327108
  83.8 2.6 %copy-start.12 = (f32[768]{0:T(1024)S(1)}, f32[768]{0:T(1024)}, u32[]{:S(2)}) copy-start(f32[768]{0:T(1024)} %param.20) | copy-start | bytes 9220
  84.2 4.7 %copy-start.5 = (bf16[384,768]{1,0:T(8,128)(2,1)S(1)}, bf16[384,768]{1,0:T(8,128)(2,1)}, u32[]{:S(2)}) copy-start(bf16[384,768]{1,0:T(8,128)(2,1)} %param.25) | copy-start | bytes 1769476
  86.9 23.5 %copy-start.10 = (f32[384]{0:T(512)S(1)}, f32[384]{0:T(512)}, u32[]{:S(2)}) copy-start(f32[384]{0:T(512)} %param.22) | copy-start | bytes 4612
  86.9 6.9 %collective-permute-start.4 = (bf16[2,3,12,384]{3,2,1,0:T(8,128)(2,1)S(1)}, bf16[2,3,12,384]{3,2,1,0:T(8,128)(2,1)S(1)}, u32[]{:S(2)}, u32[]{:S(2)}) collective-permute-start(bf16[2,3,12,384]{3,2,1,0:T(8,128)(2,1)S(1)} %get-tuple-element.153), channel_id=1, source_target_pairs={{0,32},{32,64},{64,96},{96,128},{128,160},{160,192},{192,224},{224... | collective-permute-start | bytes 165896 | tf_op jit(solution)/shard_map/ppermute | solution.py:23
  89.9 7.4 %collective-permute-start.5 = (bf16[2,3,12,384]{3,2,1,0:T(8,128)(2,1)S(1)}, bf16[2,3,12,384]{3,2,1,0:T(8,128)(2,1)S(1)}, u32[]{:S(2)}, u32[]{:S(2)}) collective-permute-start(bf16[2,3,12,384]{3,2,1,0:T(8,128)(2,1)S(1)} %get-tuple-element.152), channel_id=1, source_target_pairs={{32,0},{64,32},{96,64},{128,96},{160,128},{192,160},{224,192},{256... | collective-permute-start | bytes 165896 | tf_op jit(solution)/shard_map/ppermute | solution.py:25
  97.4 10.1 %collective-permute-start.6 = (bf16[2,12,6,384]{3,2,1,0:T(8,128)(2,1)S(1)}, bf16[2,12,6,384]{3,2,1,0:T(8,128)(2,1)S(1)}, u32[]{:S(2)}, u32[]{:S(2)}) collective-permute-start(bf16[2,12,6,384]{3,2,1,0:T(8,128)(2,1)S(1)} %get-tuple-element.148), channel_id=1, source_target_pairs={{0,1},{1,2},{2,3},{3,4},{4,5},{5,6},{6,7},{7,8},{8,9},{9,10},{10,1... | collective-permute-start | bytes 331784 | tf_op jit(solution)/shard_map/ppermute | solution.py:23
  99.4 9.9 %collective-permute-start.7 = (bf16[2,12,6,384]{3,2,1,0:T(8,128)(2,1)S(1)}, bf16[2,12,6,384]{3,2,1,0:T(8,128)(2,1)S(1)}, u32[]{:S(2)}, u32[]{:S(2)}) collective-permute-start(bf16[2,12,6,384]{3,2,1,0:T(8,128)(2,1)S(1)} %get-tuple-element.149), channel_id=1, source_target_pairs={{1,0},{2,1},{3,2},{4,3},{5,4},{6,5},{7,6},{8,7},{9,8},{10,9},{11,1... | collective-permute-start | bytes 331784 | tf_op jit(solution)/shard_map/ppermute | solution.py:25
  136.8 1.9 %copy-start.6 = (bf16[2,2,6,24,384]{4,3,2,1,0:T(8,128)(2,1)S(1)}, bf16[2,2,6,24,384]{4,3,2,1,0:T(8,128)(2,1)}, u32[]{:S(2)}) copy-start(bf16[2,2,6,24,384]{4,3,2,1,0:T(8,128)(2,1)} %get-tuple-element.273) | copy-start | bytes 1327108 | tf_op jit(solution)/shard_map/while
  138.8 0.8 copy-start.7
  165.9 1.9 %copy-start.6 = (bf16[2,2,6,24,384]{4,3,2,1,0:T(8,128)(2,1)S(1)}, bf16[2,2,6,24,384]{4,3,2,1,0:T(8,128)(2,1)}, u32[]{:S(2)}) copy-start(bf16[2,2,6,24,384]{4,3,2,1,0:T(8,128)(2,1)} %get-tuple-element.273) | copy-start | bytes 1327108 | tf_op jit(solution)/shard_map/while
  167.9 0.8 copy-start.7
  169.8 3.3 %copy-start.13 = (f32[192]{0:T(256)S(1)}, f32[192]{0:T(256)}, u32[]{:S(2)}) copy-start(f32[192]{0:T(256)} %param.26) | copy-start | bytes 2308
  169.8 4.1 %copy-start.3 = (f32[2,12,24,192]{3,2,1,0:T(8,128)S(1)}, f32[2,12,24,192]{3,2,1,0:T(8,128)}, u32[]{:S(2)}) copy-start(f32[2,12,24,192]{3,2,1,0:T(8,128)} %copy-done.2) | copy-start | bytes 1327108
  169.8 4.1 %copy-start.8 = (bf16[192,192]{1,0:T(8,128)(2,1)S(1)}, bf16[192,192]{1,0:T(8,128)(2,1)}, u32[]{:S(2)}) copy-start(bf16[192,192]{1,0:T(8,128)(2,1)} %param.27) | copy-start | bytes 221188
where the time goes:
time: 177 us; the launch traced here: 175 us
  local copies, waits for them, and re-layouts  84.8 us (48%)
  starting transfers between devices  35 us (20%)
  matrix products  28.3 us (16%)
  waiting for transfers between devices  13.2 us (7%)
  other arithmetic  12.4 us (7%)
    ppermute x4, starting transfers between devices, extended_2(): lax.ppermute(head, axis, [((i + 1) % count, i) for i in range(ends)])  24.5 us
    reshape x5, local copies, waits for them, and re-layouts, window_heads(): packed.reshape(levels // 2, 2, row_count, col_count // WIN_LON, WIN_LON,...  17.4 us
    transpose x5, local copies, waits for them, and re-layouts, window_heads(): packed = packed.transpose(0, 3, 5, 6, 1, 2, 4, 7)  16.2 us
    ppermute x4, waiting for transfers between devices, extended_2(): lax.ppermute(head, axis, [((i + 1) % count, i) for i in range(ends)])  11.5 us
    reshape x3, local copies, waits for them, and re-layouts, window_heads(): packed.reshape(levels // 2, col_count // WIN_LON, 3, head_count, window_l...  10.9 us
    ppermute x4, starting transfers between devices, extended_2(): lax.ppermute(tail, axis, [(i, (i + 1) % count) for i in range(ends)])  10.5 us
    dot_general x5, matrix products, window_heads(): jnp.einsum('abhtd,abhsd->abhts', packed[:, :, 0], packed[:, :, 1], prefer...  9.71 us
    dot_general x5, matrix products, window_heads(): jnp.einsum('abhts,abhsd->abhtd', weights, packed[:, :, 2], preferred_elem...  8.07 us
  transfers between devices with their start and end apart: 8, of which 6 were waited for; matrix products, arithmetic and copies ran while one was open for 1% of the time, Pallas kernels for 0%

commit v1 on v0

v1 whole, which is shorter than its diff:
```python
import functools

import jax
import jax.numpy as jnp
import ml_dtypes
import numpy as np
from jax import lax
from jax.experimental import pallas as pl
from jax.experimental.pallas import tpu as pltpu
from jax.sharding import PartitionSpec as P

MESH = pl.DeviceIdType.MESH
BF = jnp.bfloat16
F32 = jnp.float32
EPSILON = 1e-05
C = 192
CC = 384
ROWS, COLS = 12, 24
OWN = ROWS * COLS
UNIT = 18
WIN = 72
PAD = 80
HEAD = 32
Q_SCALE = float(HEAD**-0.5 * np.log2(np.e))
V_SCALE = 2.0**-8
FAR = -1e30
HALO = 160
LAT_AT, LON_AT, DIAG_AT = 0, 64, 128


def one_hot(rows, cols, pairs):
    out = np.zeros((rows, cols), np.float32)
    for r, c in pairs:
        out[r, c] = 1.0
    return out.astype(ml_dtypes.bfloat16)


def halo_slot(unit_of):
    for j in range(3):
        yield LAT_AT + j * UNIT, (0, j + 1)
        yield LON_AT + j * UNIT, (j + 1, 0)
    yield DIAG_AT, (0, 0)


def received(a, b):
    if a == 3 and b == 3:
        return DIAG_AT
    if a == 3:
        return LAT_AT + b * UNIT
    if b == 3:
        return LON_AT + a * UNIT
    return None


def window_row(a, b):
    return ((a // 2) * 2 + b // 2) * PAD + ((a % 2) * 2 + b % 2) * UNIT


def natural(level, r, c):
    n = r * COLS + c
    return n if level == 0 else OWN - 1 - n


@functools.cache
def tables():
    units = [(a, b) for a in range(4) for b in range(4)]
    send1, gather1, final = [], [], []
    for level in range(2):

        def own(a, b, t, level=level):
            return natural(level, a * 3 + t // 6, b * 6 + t % 6)

        send1.append(
            one_hot(HALO, OWN, [(s + t, own(a, b, t)) for s, (a, b) in halo_slot(None) for t in range(UNIT)])
        )
        pairs = []
        for a, b in units:
            slot = received(a, b)
            for t in range(UNIT):
                source = own(a + 1, b + 1, t) if slot is None else OWN + slot + t
                pairs.append((window_row(a, b) + t, source))
        gather1.append(one_hot(4 * PAD, OWN + HALO, pairs))
        pairs = []
        for r in range(ROWS):
            for c in range(COLS):
                qr, qc = int(r < 6), int(c < 12)
                y, x = r % 6, c % 12
                k = y % 2 + 2 * (x % 2)
                t = (y // 2) * 6 + x // 2
                pairs.append((natural(level, r, c), (qr * 2 + qc) * PAD + k * UNIT + t))
        final.append(one_hot(OWN, 4 * PAD, pairs))
    send2 = one_hot(
        HALO, 4 * PAD, [(s + t, window_row(a, b) + t) for s, (a, b) in halo_slot(None) for t in range(UNIT)]
    )
    pairs = []
    for y in range(ROWS):
        for x in range(COLS):
            a, b, t = y // 3, x // 6, (y % 3) * 6 + x % 6
            slot = received(a, b)
            source = window_row(a + 1, b + 1) + t if slot is None else 4 * PAD + slot + t
            k = y % 2 + 2 * (x % 2)
            i, j = y // 2, x // 2
            cell = ((i // 3) * 2 + j // 6) * UNIT + (i % 3) * 6 + j % 6
            pairs.append((k * PAD + cell, source))
    gather2 = one_hot(4 * PAD, 4 * PAD + HALO, pairs)
    pairs = []
    for quarter in range(4):
        for k in range(4):
            for t in range(UNIT):
                pairs.append((quarter * PAD + k * UNIT + t, k * PAD + quarter * UNIT + t))
    send3 = one_hot(4 * PAD, 4 * PAD, pairs)
    ones4 = np.zeros((4 * PAD, 128), np.float32)
    ones2 = np.zeros((2 * PAD, 128), np.float32)
    for h in range(4):
        ones4[h * PAD : h * PAD + WIN, h * HEAD : (h + 1) * HEAD] = 1.0
    for h in range(2):
        ones2[h * PAD : h * PAD + WIN, h * HEAD : (h + 1) * HEAD] = 1.0
    ones2[0:WIN, 2 * HEAD :] = 1.0
    side_q = np.arange(PAD) >= WIN // 2
    side_k = np.arange(4 * PAD) % PAD >= WIN // 2
    far = np.where(side_q[:, None] != side_k[None, :], np.float32(FAR), np.float32(0.0))
    heads = np.zeros((16, 4, 128), np.float32)
    for h in range(4):
        heads[:, h, h * HEAD : (h + 1) * HEAD] = 1.0
    return dict(
        send1=np.stack(send1),
        gather1=np.stack(gather1),
        send2=send2,
        gather2=gather2,
        send3=send3,
        final=np.stack(final),
        ones4=ones4.astype(ml_dtypes.bfloat16),
        ones2=ones2.astype(ml_dtypes.bfloat16),
        far=far.astype(np.float32),
    )


ARGUMENTS = ("tokens", "norm_gain", "qkv_weight", "proj_weight", "merge_gain", "merge_weight", "coarse_gain", "coarse_qkv")
ARGUMENTS += ("coarse_proj", "up_weight", "up_gain", "out_weight")
TABLES = ("send1", "gather1", "send2", "gather2", "send3", "final", "ones4", "ones2", "far")


def dot(a, b):
    return jnp.dot(a, b, preferred_element_type=F32)


def norm(values, gain):
    average = jnp.mean(values, axis=-1, keepdims=True)
    centred = values - average
    spread = jnp.mean(centred * centred, axis=-1, keepdims=True)
    return (centred * lax.rsqrt(spread + EPSILON) * gain).astype(BF)


def attend(q, k, v, ones, masks, far):
    count = ones.shape[0] // PAD
    keys = jnp.concatenate([k * m for m in masks[:count]], axis=0)
    scores = lax.dot_general(q, keys, (((1,), (1,)), ((), ())), preferred_element_type=F32)
    if far is not None:
        scores = scores + far
    raised = jnp.exp2(scores).astype(BF)
    small = v * jnp.bfloat16(V_SCALE)
    values = jnp.concatenate([small * m for m in masks[:count]], axis=0)
    total = dot(raised, ones)
    return dot(raised, values) / (total * V_SCALE)


def kernel(lat_n, lon_n, *refs):
    names = list(ARGUMENTS)
    names += list(TABLES)
    hbm = dict(zip(names, refs))
    out_ref = refs[len(names)]
    scratch = refs[len(names) + 1 :]
    vm = dict(zip(names[1:], scratch))
    (qkv_pad, up_pad, far_v, buf1, buf2, buf3, snd1, snd2, snd3, load_sem, tok_sem, send_sem, recv_sem) = scratch[
        len(names) - 1 :
    ]

    lat, lon = lax.axis_index("lat"), lax.axis_index("lon")
    up, down = lax.rem(lat + 1, lat_n), lax.rem(lat + lat_n - 1, lat_n)
    east, west = lax.rem(lon + 1, lon_n), lax.rem(lon + lon_n - 1, lon_n)
    fore = ((up, lon), (lat, east), (up, east))
    back = ((down, lon), (lat, west), (down, west))

    barrier = pltpu.get_barrier_semaphore()
    for device in fore + back:
        pl.semaphore_signal(barrier, inc=1, device_id=device, device_id_type=MESH)

    loads = {}
    for level in range(2):
        loads["tokens", level] = pltpu.make_async_copy(
            hbm["tokens"].at[level], buf1.at[level, pl.ds(0, OWN)], tok_sem.at[level]
        )
        loads["tokens", level].start()
    order = ["send1", "gather1", "norm_gain", "qkv_weight", "ones4", "ones2", "far", "proj_weight", "send2", "gather2"]
    order += [n for n in names[1:] if n not in order]
    for i, n in enumerate(order):
        loads[n] = pltpu.make_async_copy(hbm[n], vm[n], load_sem.at[i])
        loads[n].start()

    def need(*wanted):
        for n in wanted:
            loads.pop(n).wait()

    def exchange(stage, level, source, target, starts, rows):
        forward = (level == 1) if stage < 2 else (level == 0)
        copies = []
        for i, device in enumerate(fore if forward else back):
            piece = pl.ds(starts[i][0], rows[i])
            place = pl.ds(starts[i][1], rows[i])
            copy = pltpu.make_async_remote_copy(
                src_ref=source.at[level, piece],
                dst_ref=target.at[level, place],
                send_sem=send_sem.at[stage, level, i],
                recv_sem=recv_sem.at[stage, level, i],
                device_id=device,
                device_id_type=MESH,
            )
            copy.start()
            copies.append(copy)
        return copies

    halo_rows = (64, 64, 32)

    def halo_starts(base):
        return ((LAT_AT, base + LAT_AT), (LON_AT, base + LON_AT), (DIAG_AT, base + DIAG_AT))

    need("send1")
    for level in range(2):
        need(("tokens", level))
        snd1[level] = dot(vm["send1"][level], buf1[level, 0:OWN]).astype(BF)
    pl.semaphore_wait(barrier, 6)
    one = [exchange(0, level, snd1, buf1, halo_starts(OWN), halo_rows) for level in range(2)]

    need("qkv_weight", "far")
    zero = jnp.zeros((C, 64), BF)
    for part in range(3):
        qkv_pad[:, part * 256 : part * 256 + C] = vm["qkv_weight"][:, part * C : (part + 1) * C]
        qkv_pad[:, part * 256 + C : (part + 1) * 256] = zero
    edge = (lat_n - 1, 0)
    for level in range(2):
        far_v[level] = jnp.where(lat == edge[level], vm["far"][...], 0.0)
    need("norm_gain", "ones4", "ones2", "proj_weight", "gather1")
    lane = lax.broadcasted_iota(jnp.int32, (PAD, 128), 1)
    masks = [jnp.where(lane // HEAD == h, 1.0, 0.0).astype(BF) for h in range(4)]
    ones4, ones2 = vm["ones4"], vm["ones2"]

    def fine(tokens, level, windows):
        normed = norm(tokens, vm["norm_gain"][...])
        packed = dot(normed, qkv_pad[...])
        q = (packed[:, 0:256] * Q_SCALE).astype(BF)
        k = packed[:, 256:512].astype(BF)
        v = packed[:, 512:768].astype(BF)
        heads = []
        for i, w in enumerate(windows):
            at = slice(i * PAD, (i + 1) * PAD)
            far = far_v[level[i]] if w >= 2 else None
            a = attend(q[at, 0:128], k[at, 0:128], v[at, 0:128], ones4[...], masks, far)
            far2 = far[:, 0 : 2 * PAD] if w >= 2 else None
            b = attend(q[at, 128:256], k[at, 128:256], v[at, 128:256], ones2[...], masks, far2)
            heads.append(jnp.concatenate([a, b], axis=1).astype(BF))
        heads = jnp.concatenate(heads, axis=0)[:, 0:C]
        result = (tokens + dot(heads, vm["proj_weight"][...])).astype(BF)
        for i, w in enumerate(windows):
            buf2[level[i], w * PAD : (w + 1) * PAD] = result[i * PAD : (i + 1) * PAD]

    first = [dot(vm["gather1"][level, 0:PAD, 0:OWN], buf1[level, 0:OWN]) for level in range(2)]
    fine(jnp.concatenate(first, axis=0), (0, 1), (0, 0))

    need("send2")
    two = []
    for level in range(2):
        for copy in one[level]:
            copy.wait_recv()
        rest = dot(vm["gather1"][level, PAD : 4 * PAD], buf1[level])
        fine(rest, (level,) * 3, (1, 2, 3))
        snd2[level] = dot(vm["send2"][...], buf2[level, 0 : 4 * PAD]).astype(BF)
        two.append(exchange(1, level, snd2, buf2, halo_starts(4 * PAD), halo_rows))

    need("up_weight")
    for k in range(4):
        up_pad[:, k * 256 : k * 256 + C] = vm["up_weight"][:, k * C : (k + 1) * C]
    need("gather2", "send3", "merge_gain", "merge_weight", "coarse_gain", "coarse_qkv", "coarse_proj")
    need("up_gain", "out_weight", "final")

    three = []
    for level in range(2):
        for copy in two[level]:
            copy.wait_recv()
        cells = dot(vm["gather2"][...], buf2[level])
        group = [cells[k * PAD : (k + 1) * PAD] for k in range(4)]
        column = [k if level == 0 else 3 - k for k in range(4)]
        average = jnp.sum(group[0] + group[1] + group[2] + group[3], axis=-1, keepdims=True) * (1.0 / (4 * C))
        centred = [g - average for g in group]
        squares = [c * c for c in centred]
        spread = jnp.sum(squares[0] + squares[1] + squares[2] + squares[3], axis=-1, keepdims=True) * (1.0 / (4 * C))
        scale = lax.rsqrt(spread + EPSILON)
        coarse = jnp.zeros((PAD, CC), F32)
        for k in range(4):
            stacked = (centred[k] * scale * vm["merge_gain"][column[k] : column[k] + 1]).astype(BF)
            coarse = coarse + dot(stacked, vm["merge_weight"][column[k] * C : (column[k] + 1) * C])
        coarse = coarse.astype(BF).astype(F32)
        normed = norm(coarse, vm["coarse_gain"][...])
        packed = dot(normed, vm["coarse_qkv"][...])
        heads = []
        for j in range(3):
            q = (packed[:, j * 128 : (j + 1) * 128] * Q_SCALE).astype(BF)
            k = packed[:, CC + j * 128 : CC + (j + 1) * 128].astype(BF)
            v = packed[:, 2 * CC + j * 128 : 2 * CC + (j + 1) * 128].astype(BF)
            heads.append(attend(q, k, v, ones4[...], masks, far_v[level]).astype(BF))
        heads = jnp.concatenate(heads, axis=1)
        coarse_out = (coarse + dot(heads, vm["coarse_proj"][...])).astype(BF)
        normed = []
        for k in range(4):
            lifted = dot(coarse_out, up_pad[:, column[k] * 256 : column[k] * 256 + C])
            normed.append(norm(lifted, vm["up_gain"][...]))
        branch = dot(jnp.concatenate(normed, axis=0), vm["out_weight"][...])
        encoded = (cells + branch).astype(BF)
        quarters = dot(vm["send3"][...], encoded).astype(BF)
        buf3[level, 0:PAD] = quarters[0:PAD]
        snd3[level] = quarters[PAD : 4 * PAD]
        places = ((PAD, 2 * PAD), (0, PAD), (2 * PAD, 3 * PAD))
        three.append(exchange(2, level, snd3, buf3, places, (PAD, PAD, PAD)))

    for level in range(2):
        for copy in three[level]:
            copy.wait_recv()
        out_ref[level] = dot(vm["final"][level], buf3[level]).astype(BF)
    for copies in one + two + three:
        for copy in copies:
            copy.wait_send()


def body(lat_n, lon_n, tokens, norm_gain, qkv_weight, proj_weight, merge_gain, merge_weight, coarse_gain, *rest):
    coarse_qkv, coarse_proj, up_weight, up_gain, out_weight = rest
    table = tables()
    args = [
        tokens.reshape(2, OWN, C),
        norm_gain.reshape(1, C),
        qkv_weight,
        proj_weight,
        merge_gain.reshape(4, C),
        merge_weight,
        coarse_gain.reshape(1, CC),
        coarse_qkv,
        coarse_proj,
        up_weight,
        up_gain.reshape(1, C),
        out_weight,
    ] + [jnp.asarray(table[n]) for n in TABLES]
    scratch = [pltpu.VMEM(a.shape, a.dtype) for a in args[1:]]
    scratch += [
        pltpu.VMEM((C, 768), BF),
        pltpu.VMEM((CC, 1024), BF),
        pltpu.VMEM((2, PAD, 4 * PAD), F32),
        pltpu.VMEM((2, OWN + HALO, C), BF),
        pltpu.VMEM((2, 4 * PAD + HALO, C), BF),
        pltpu.VMEM((2, 4 * PAD, C), BF),
        pltpu.VMEM((2, HALO, C), BF),
        pltpu.VMEM((2, HALO, C), BF),
        pltpu.VMEM((2, 3 * PAD, C), BF),
        pltpu.SemaphoreType.DMA((len(args) - 1,)),
        pltpu.SemaphoreType.DMA((2,)),
        pltpu.SemaphoreType.DMA((3, 2, 3)),
        pltpu.SemaphoreType.DMA((3, 2, 3)),
    ]
    out = pl.pallas_call(
        functools.partial(kernel, lat_n, lon_n),
        out_shape=jax.ShapeDtypeStruct((2, OWN, C), BF),
        in_specs=[pl.BlockSpec(memory_space=pl.ANY)] * len(args),
        out_specs=pl.BlockSpec(memory_space=pltpu.VMEM),
        scratch_shapes=scratch,
        compiler_params=pltpu.CompilerParams(
            collective_id=0, has_side_effects=True, vmem_limit_bytes=48 * 1024 * 1024
        ),
    )(*args)
    return out.reshape(tokens.shape)


def solution(mesh):
    placed = (P(None, "lat", "lon", None),) + (P(),) * 11
    return jax.shard_map(
        functools.partial(body, mesh.shape["lat"], mesh.shape["lon"]),
        mesh=mesh,
        in_specs=placed,
        out_specs=P(None, "lat", "lon", None),
        check_vma=False,
    )
```

time: 177 us -> 54.7 us (0.31)
  local copies, waits for them, and re-layouts: 84.8 us -> 18.5 us
  Pallas kernels: 0 us -> 35.4 us
  starting transfers between devices: 35 us -> 0 us
  matrix products: 28.3 us -> 0 us
  waiting for transfers between devices: 13.2 us -> 0 us
  other arithmetic: 12.4 us -> 0 us
    pallas_call x0 -> x1, Pallas kernels: none -> 35.4 us  [body(): pl.pallas_call(functools.partial(kernel, lat_n, lon_n), out_shape=jax.Sha...]
    ppermute x8 -> x0, starting transfers between devices: 35 us -> none  [the longest x4 24.5 us: extended_2(): lax.ppermute(head, axis, [((i + 1) % count, i) for i in range(ends)])]
    reshape x12 -> x2, local copies, waits for them, and re-layouts: 29 us -> 0.08 us  [the longest x1 0.08 us: body(): merge_gain.reshape(4, C)]
    dot_general x19 -> x0, matrix products: 28.3 us -> none  [the longest x5 9.71 us: window_heads(): jnp.einsum('abhtd,abhsd->abhts', packed[:, :, 0], packed[:, :, 1], prefer...]
    transpose x11 -> x0, local copies, waits for them, and re-layouts: 18.8 us -> none  [the longest x5 16.2 us: window_heads(): packed = packed.transpose(0, 3, 5, 6, 1, 2, 4, 7)]
    unnamed x29 -> x43, local copies, waits for them, and re-layouts: 2.16 us -> 18.4 us
    ppermute x8 -> x0, waiting for transfers between devices: 13.2 us -> none  [the longest x4 11.5 us: extended_2(): lax.ppermute(head, axis, [((i + 1) % count, i) for i in range(ends)])]
    while x15 -> x0, local copies, waits for them, and re-layouts: 9.05 us -> none
  transfers between devices with their start and end apart: 8 -> 0, of which waited for: 6 -> 0; matrix products, arithmetic and copies ran while one was open for 1% -> 0% of each run, Pallas kernels for 0% -> 0%
where the time goes in v1:
time: 54.7 us; the launch traced here: 54 us
  Pallas kernels  35.4 us (65%)
  local copies, waits for them, and re-layouts  18.5 us (34%)
    pallas_call x1, Pallas kernels, body(): pl.pallas_call(functools.partial(kernel, lat_n, lon_n), out_shape=jax.Sha...  35.4 us
    unnamed x43, local copies, waits for them, and re-layouts  18.4 us

profile of v1, /device:TPU:24, one launch (start us, length us, event | category | flops | bytes accessed | tf_op | source)
XLA Modules:
  0.0 54.0 jit_solution(8232211738253426287)
XLA Ops:
  0.0 0.0 copy-start.20
  0.0 0.0 copy-start.19
  0.0 0.7 %copy-done.20 = f32[384]{0:T(512)S(1)} copy-done((f32[384]{0:T(512)S(1)}, f32[384]{0:T(512)}, u32[]{:S(2)}) %copy-start.20) | copy-done | bytes 1560
  0.7 0.0 copy-done.19
  0.7 0.0 copy-start.17
  0.7 0.0 copy-start.18
  0.7 0.1 reshape.20.refs_4_
  0.8 0.6 %copy-done.17 = f32[192]{0:T(256)S(1)} copy-done((f32[192]{0:T(256)S(1)}, f32[192]{0:T(256)}, u32[]{:S(2)}) %copy-start.17) | copy-done | bytes 792
  1.4 0.0 copy-done.18
  1.4 0.0 copy-start
  1.4 1.2 %copy-done = bf16[384,1152]{1,0:T(8,128)(2,1)S(1)} copy-done((bf16[384,1152]{1,0:T(8,128)(2,1)S(1)}, bf16[384,1152]{1,0:T(8,128)(2,1)}, u32[]{:S(2)}) %copy-start) | copy-done | bytes 884760
  2.6 0.0 copy-start.1
  2.6 1.1 %copy-done.1 = bf16[2,320,448]{2,1,0:T(8,128)(2,1)S(1)} copy-done((bf16[2,320,448]{2,1,0:T(8,128)(2,1)S(1)}, bf16[2,320,448]{2,1,0:T(8,128)(2,1)}, u32[]{:S(2)}) %copy-start.1) | copy-done | bytes 573464
  3.7 0.0 copy-start.2
  3.7 1.1 %copy-done.2 = bf16[768,384]{1,0:T(8,128)(2,1)S(1)} copy-done((bf16[768,384]{1,0:T(8,128)(2,1)S(1)}, bf16[768,384]{1,0:T(8,128)(2,1)}, u32[]{:S(2)}) %copy-start.2) | copy-done | bytes 589848
  4.7 0.0 copy-start.3
  4.7 1.1 %copy-done.3 = bf16[384,768]{1,0:T(8,128)(2,1)S(1)} copy-done((bf16[384,768]{1,0:T(8,128)(2,1)S(1)}, bf16[384,768]{1,0:T(8,128)(2,1)}, u32[]{:S(2)}) %copy-start.3) | copy-done | bytes 589848
  5.8 0.0 copy-start.4
  5.8 1.0 %copy-done.4 = bf16[2,288,320]{2,1,0:T(8,128)(2,1)S(1)} copy-done((bf16[2,288,320]{2,1,0:T(8,128)(2,1)S(1)}, bf16[2,288,320]{2,1,0:T(8,128)(2,1)}, u32[]{:S(2)}) %copy-start.4) | copy-done | bytes 368664
  6.8 0.0 copy-start.5
  6.8 1.0 %copy-done.5 = bf16[320,480]{1,0:T(8,128)(2,1)S(1)} copy-done((bf16[320,480]{1,0:T(8,128)(2,1)S(1)}, bf16[320,480]{1,0:T(8,128)(2,1)}, u32[]{:S(2)}) %copy-start.5) | copy-done | bytes 307224
  7.8 0.0 copy-start.6
  7.8 1.0 %copy-done.6 = bf16[2,12,24,192]{3,2,1,0:T(8,128)(2,1)S(1)} copy-done((bf16[2,12,24,192]{3,2,1,0:T(8,128)(2,1)S(1)}, bf16[2,12,24,192]{3,2,1,0:T(8,128)(2,1)}, u32[]{:S(2)}) %copy-start.6) | copy-done | bytes 221208
  8.7 0.0 copy-start.7
  8.7 1.0 %copy-done.7 = bf16[384,384]{1,0:T(8,128)(2,1)S(1)} copy-done((bf16[384,384]{1,0:T(8,128)(2,1)S(1)}, bf16[384,384]{1,0:T(8,128)(2,1)}, u32[]{:S(2)}) %copy-start.7) | copy-done | bytes 294936
  9.7 0.0 copy-start.8
  9.7 0.9 %copy-done.8 = bf16[192,576]{1,0:T(8,128)(2,1)S(1)} copy-done((bf16[192,576]{1,0:T(8,128)(2,1)S(1)}, bf16[192,576]{1,0:T(8,128)(2,1)}, u32[]{:S(2)}) %copy-start.8) | copy-done | bytes 221208
  10.6 0.0 copy-start.9
  10.6 0.9 %copy-done.9 = bf16[320,320]{1,0:T(8,128)(2,1)S(1)} copy-done((bf16[320,320]{1,0:T(8,128)(2,1)S(1)}, bf16[320,320]{1,0:T(8,128)(2,1)}, u32[]{:S(2)}) %copy-start.9) | copy-done | bytes 204824
  11.6 0.0 copy-start.10
  11.6 0.9 %copy-done.10 = bf16[2,160,288]{2,1,0:T(8,128)(2,1)S(1)} copy-done((bf16[2,160,288]{2,1,0:T(8,128)(2,1)S(1)}, bf16[2,160,288]{2,1,0:T(8,128)(2,1)}, u32[]{:S(2)}) %copy-start.10) | copy-done | bytes 184344
  12.5 0.0 copy-start.11
  12.5 0.9 %copy-done.11 = f32[80,320]{1,0:T(8,128)S(1)} copy-done((f32[80,320]{1,0:T(8,128)S(1)}, f32[80,320]{1,0:T(8,128)}, u32[]{:S(2)}) %copy-start.11) | copy-done | bytes 102424
  13.4 0.0 copy-start.12
  13.4 0.9 %copy-done.12 = bf16[160,320]{1,0:T(8,128)(2,1)S(1)} copy-done((bf16[160,320]{1,0:T(8,128)(2,1)S(1)}, bf16[160,320]{1,0:T(8,128)(2,1)}, u32[]{:S(2)}) %copy-start.12) | copy-done | bytes 102424
  14.3 0.0 copy-start.13
  14.3 0.9 %copy-done.13 = bf16[192,192]{1,0:T(8,128)(2,1)S(1)} copy-done((bf16[192,192]{1,0:T(8,128)(2,1)S(1)}, bf16[192,192]{1,0:T(8,128)(2,1)}, u32[]{:S(2)}) %copy-start.13) | copy-done | bytes 73752
  15.2 0.0 copy-start.14
  15.2 0.9 %copy-done.14 = bf16[192,192]{1,0:T(8,128)(2,1)S(1)} copy-done((bf16[192,192]{1,0:T(8,128)(2,1)S(1)}, bf16[192,192]{1,0:T(8,128)(2,1)}, u32[]{:S(2)}) %copy-start.14) | copy-done | bytes 73752
  16.1 0.0 copy-start.15
  16.1 0.9 %copy-done.15 = bf16[320,128]{1,0:T(8,128)(2,1)S(1)} copy-done((bf16[320,128]{1,0:T(8,128)(2,1)S(1)}, bf16[320,128]{1,0:T(8,128)(2,1)}, u32[]{:S(2)}) %copy-start.15) | copy-done | bytes 81944
  17.0 0.0 copy-start.16
  17.0 0.8 %copy-done.16 = bf16[160,128]{1,0:T(8,128)(2,1)S(1)} copy-done((bf16[160,128]{1,0:T(8,128)(2,1)S(1)}, bf16[160,128]{1,0:T(8,128)(2,1)}, u32[]{:S(2)}) %copy-start.16) | copy-done | bytes 40984
  17.8 35.4 %shard_map.199 = bf16[2,288,192]{2,1,0:T(8,128)(2,1)S(1)} custom-call(bf16[2,288,192]{2,1,0:T(8,128)(2,1)S(1)} %bitcast.5, f32[1,192]{1,0:T(1,128)S(1)} %bitcast.6, bf16[192,576]{1,0:T(8,128)(2,1)S(1)} %copy-done.8, bf16[192,192]{1,0:T(8,128)(2,1)S(1)} %copy-done.13, f32[4,192]{1,0:T(4,128)S(1)} %reshape.20.refs_4_, bf16[768,384]{1,0:T(8,128)(2,1)S(1)} %copy-done.2, ...), custom_call_target="tpu_custom_call" | custom-call | tf_op jit(solution)/shard_map/pallas_call | solution.py:366
  53.2 0.7 %copy.23 = bf16[2,12,24,192]{3,2,1,0:T(8,128)(2,1)} copy(bf16[2,12,24,192]{3,2,1,0:T(8,128)(2,1)S(1)} %bitcast.4) | data formatting | bytes 442368
  (1 shorter events, 0.0 us)
Async XLA Ops:
  0.0 0.7 %copy-start.20 = (f32[384]{0:T(512)S(1)}, f32[384]{0:T(512)}, u32[]{:S(2)}) copy-start(f32[384]{0:T(512)} %param.27) | copy-start | bytes 4612
  0.0 0.7 %copy-start.19 = (f32[768]{0:T(1024)S(1)}, f32[768]{0:T(1024)}, u32[]{:S(2)}) copy-start(f32[768]{0:T(1024)} %param.25) | copy-start | bytes 9220
  0.7 0.7 %copy-start.17 = (f32[192]{0:T(256)S(1)}, f32[192]{0:T(256)}, u32[]{:S(2)}) copy-start(f32[192]{0:T(256)} %param.22) | copy-start | bytes 2308
  0.7 0.7 %copy-start.18 = (f32[192]{0:T(256)S(1)}, f32[192]{0:T(256)}, u32[]{:S(2)}) copy-start(f32[192]{0:T(256)} %param.31) | copy-start | bytes 2308
  1.4 1.2 %copy-start = (bf16[384,1152]{1,0:T(8,128)(2,1)S(1)}, bf16[384,1152]{1,0:T(8,128)(2,1)}, u32[]{:S(2)}) copy-start(bf16[384,1152]{1,0:T(8,128)(2,1)} %refs_7_.1) | copy-start | bytes 2654212
  2.6 1.1 %copy-start.1 = (bf16[2,320,448]{2,1,0:T(8,128)(2,1)S(1)}, bf16[2,320,448]{2,1,0:T(8,128)(2,1)}, u32[]{:S(2)}) copy-start(bf16[2,320,448]{2,1,0:T(8,128)(2,1)} %constant.19.clone.refs_13_) | copy-start | bytes 1720324
  3.7 1.1 %copy-start.2 = (bf16[768,384]{1,0:T(8,128)(2,1)S(1)}, bf16[768,384]{1,0:T(8,128)(2,1)}, u32[]{:S(2)}) copy-start(bf16[768,384]{1,0:T(8,128)(2,1)} %refs_5_.1) | copy-start | bytes 1769476
  4.7 1.1 %copy-start.3 = (bf16[384,768]{1,0:T(8,128)(2,1)S(1)}, bf16[384,768]{1,0:T(8,128)(2,1)}, u32[]{:S(2)}) copy-start(bf16[384,768]{1,0:T(8,128)(2,1)} %refs_9_.1) | copy-start | bytes 1769476
  5.8 1.0 %copy-start.4 = (bf16[2,288,320]{2,1,0:T(8,128)(2,1)S(1)}, bf16[2,288,320]{2,1,0:T(8,128)(2,1)}, u32[]{:S(2)}) copy-start(bf16[2,288,320]{2,1,0:T(8,128)(2,1)} %constant.23.clone.refs_17_) | copy-start | bytes 1105924
  6.8 1.0 %copy-start.5 = (bf16[320,480]{1,0:T(8,128)(2,1)S(1)}, bf16[320,480]{1,0:T(8,128)(2,1)}, u32[]{:S(2)}) copy-start(bf16[320,480]{1,0:T(8,128)(2,1)} %constant.21.clone.refs_15_) | copy-start | bytes 921604
  7.8 1.0 %copy-start.6 = (bf16[2,12,24,192]{3,2,1,0:T(8,128)(2,1)S(1)}, bf16[2,12,24,192]{3,2,1,0:T(8,128)(2,1)}, u32[]{:S(2)}) copy-start(bf16[2,12,24,192]{3,2,1,0:T(8,128)(2,1)} %param.21) | copy-start | bytes 663556
  8.7 1.0 %copy-start.7 = (bf16[384,384]{1,0:T(8,128)(2,1)S(1)}, bf16[384,384]{1,0:T(8,128)(2,1)}, u32[]{:S(2)}) copy-start(bf16[384,384]{1,0:T(8,128)(2,1)} %refs_8_.1) | copy-start | bytes 884740
  9.7 0.9 %copy-start.8 = (bf16[192,576]{1,0:T(8,128)(2,1)S(1)}, bf16[192,576]{1,0:T(8,128)(2,1)}, u32[]{:S(2)}) copy-start(bf16[192,576]{1,0:T(8,128)(2,1)} %refs_2_.1) | copy-start | bytes 663556
  10.6 0.9 %copy-start.9 = (bf16[320,320]{1,0:T(8,128)(2,1)S(1)}, bf16[320,320]{1,0:T(8,128)(2,1)}, u32[]{:S(2)}) copy-start(bf16[320,320]{1,0:T(8,128)(2,1)} %constant.22.clone.refs_16_) | copy-start | bytes 614404
  11.6 0.9 %copy-start.10 = (bf16[2,160,288]{2,1,0:T(8,128)(2,1)S(1)}, bf16[2,160,288]{2,1,0:T(8,128)(2,1)}, u32[]{:S(2)}) copy-start(bf16[2,160,288]{2,1,0:T(8,128)(2,1)} %constant.18.clone.refs_12_) | copy-start | bytes 552964
  12.5 0.9 %copy-start.11 = (f32[80,320]{1,0:T(8,128)S(1)}, f32[80,320]{1,0:T(8,128)}, u32[]{:S(2)}) copy-start(f32[80,320]{1,0:T(8,128)} %constant.26.clone.refs_20_) | copy-start | bytes 307204
  13.4 0.9 %copy-start.12 = (bf16[160,320]{1,0:T(8,128)(2,1)S(1)}, bf16[160,320]{1,0:T(8,128)(2,1)}, u32[]{:S(2)}) copy-start(bf16[160,320]{1,0:T(8,128)(2,1)} %constant.20.clone.refs_14_) | copy-start | bytes 307204
  14.3 0.9 %copy-start.13 = (bf16[192,192]{1,0:T(8,128)(2,1)S(1)}, bf16[192,192]{1,0:T(8,128)(2,1)}, u32[]{:S(2)}) copy-start(bf16[192,192]{1,0:T(8,128)(2,1)} %refs_3_.1) | copy-start | bytes 221188
  15.2 0.9 %copy-start.14 = (bf16[192,192]{1,0:T(8,128)(2,1)S(1)}, bf16[192,192]{1,0:T(8,128)(2,1)}, u32[]{:S(2)}) copy-start(bf16[192,192]{1,0:T(8,128)(2,1)} %refs_11_.1) | copy-start | bytes 221188
  16.1 0.9 %copy-start.15 = (bf16[320,128]{1,0:T(8,128)(2,1)S(1)}, bf16[320,128]{1,0:T(8,128)(2,1)}, u32[]{:S(2)}) copy-start(bf16[320,128]{1,0:T(8,128)(2,1)} %constant.24.clone.refs_18_) | copy-start | bytes 245764
  17.0 0.8 %copy-start.16 = (bf16[160,128]{1,0:T(8,128)(2,1)S(1)}, bf16[160,128]{1,0:T(8,128)(2,1)}, u32[]{:S(2)}) copy-start(bf16[160,128]{1,0:T(8,128)(2,1)} %constant.25.clone.refs_19_) | copy-start | bytes 122884

commit v2 on v1

--- a/solution.py
+++ b/solution.py
@@ -201,6 +201,9 @@
         for n in wanted:
             loads.pop(n).wait()
 
+    def row(n):
+        return vm[n][...].reshape(1, -1)
+
     def exchange(stage, level, source, target, starts, rows):
         forward = (level == 1) if stage < 2 else (level == 0)
         copies = []
@@ -245,7 +248,7 @@
     ones4, ones2 = vm["ones4"], vm["ones2"]
 
     def fine(tokens, level, windows):
-        normed = norm(tokens, vm["norm_gain"][...])
+        normed = norm(tokens, row("norm_gain"))
         packed = dot(normed, qkv_pad[...])
         q = (packed[:, 0:256] * Q_SCALE).astype(BF)
         k = packed[:, 256:512].astype(BF)
@@ -296,10 +299,10 @@
         scale = lax.rsqrt(spread + EPSILON)
         coarse = jnp.zeros((PAD, CC), F32)
         for k in range(4):
-            stacked = (centred[k] * scale * vm["merge_gain"][column[k] : column[k] + 1]).astype(BF)
+            stacked = (centred[k] * scale * row("merge_gain")[:, column[k] * C : (column[k] + 1) * C]).astype(BF)
             coarse = coarse + dot(stacked, vm["merge_weight"][column[k] * C : (column[k] + 1) * C])
         coarse = coarse.astype(BF).astype(F32)
-        normed = norm(coarse, vm["coarse_gain"][...])
+        normed = norm(coarse, row("coarse_gain"))
         packed = dot(normed, vm["coarse_qkv"][...])
         heads = []
         for j in range(3):
@@ -312,7 +315,7 @@
         normed = []
         for k in range(4):
             lifted = dot(coarse_out, up_pad[:, column[k] * 256 : column[k] * 256 + C])
-            normed.append(norm(lifted, vm["up_gain"][...]))
+            normed.append(norm(lifted, row("up_gain")))
         branch = dot(jnp.concatenate(normed, axis=0), vm["out_weight"][...])
         encoded = (cells + branch).astype(BF)
         quarters = dot(vm["send3"][...], encoded).astype(BF)
@@ -335,16 +338,16 @@
     table = tables()
     args = [
         tokens.reshape(2, OWN, C),
-        norm_gain.reshape(1, C),
+        norm_gain,
         qkv_weight,
         proj_weight,
-        merge_gain.reshape(4, C),
+        merge_gain,
         merge_weight,
-        coarse_gain.reshape(1, CC),
+        coarse_gain,
         coarse_qkv,
         coarse_proj,
         up_weight,
-        up_gain.reshape(1, C),
+        up_gain,
         out_weight,
     ] + [jnp.asarray(table[n]) for n in TABLES]
     scratch = [pltpu.VMEM(a.shape, a.dtype) for a in args[1:]]
@@ -366,13 +369,13 @@
     out = pl.pallas_call(
         functools.partial(kernel, lat_n, lon_n),
         out_shape=jax.ShapeDtypeStruct((2, OWN, C), BF),
-        in_specs=[pl.BlockSpec(memory_space=pl.ANY)] * len(args),
+        in_specs=[pl.BlockSpec(memory_space=pltpu.HBM)] * len(args),
         out_specs=pl.BlockSpec(memory_space=pltpu.VMEM),
         scratch_shapes=scratch,
         compiler_params=pltpu.CompilerParams(
-            collective_id=0, has_side_effects=True, vmem_limit_bytes=48 * 1024 * 1024
+            collective_id=0, has_side_effects=True, vmem_limit_bytes=40 * 1024 * 1024
         ),
-    )(*args)
+    )(*[pltpu.with_memory_space_constraint(a, pltpu.HBM) for a in args])
     return out.reshape(tokens.shape)
 
 

time: 54.7 us -> 35.9 us (0.66); the launches traced: 54 us -> 35.8 us
  local copies, waits for them, and re-layouts: 18.5 us -> 0.72 us
    unnamed x43 -> x1, local copies, waits for them, and re-layouts: 18.4 us -> 0.72 us
where the time goes in v2:
time: 35.9 us; the launch traced here: 35.8 us
  Pallas kernels  35 us (97%)
  local copies, waits for them, and re-layouts  0.72 us (2%)
    pallas_call x1, Pallas kernels, body(): pl.pallas_call(functools.partial(kernel, lat_n, lon_n), out_shape=jax.Sha...  35 us

profile of v2, /device:TPU:24, one launch (start us, length us, event | category | flops | bytes accessed | tf_op | source)
XLA Modules:
  0.0 35.8 jit_solution(4496575890812051186)
XLA Ops:
  0.0 35.0 %shard_map.199 = bf16[2,288,192]{2,1,0:T(8,128)(2,1)S(1)} custom-call(bf16[2,288,192]{2,1,0:T(8,128)(2,1)} %bitcast.3, f32[192]{0:T(256)} %refs_1_.1, bf16[192,576]{1,0:T(8,128)(2,1)} %refs_2_.1, bf16[192,192]{1,0:T(8,128)(2,1)} %refs_3_.1, f32[768]{0:T(1024)} %refs_4_.1, bf16[768,384]{1,0:T(8,128)(2,1)} %refs_5_.1, f32[384]{0:T(512)} %refs_6_.1, ...), custom_call_target="tpu_custom_call" | custom-call | tf_op jit(solution)/shard_map/pallas_call | solution.py:369
  35.1 0.7 %copy.23 = bf16[2,12,24,192]{3,2,1,0:T(8,128)(2,1)} copy(bf16[2,12,24,192]{3,2,1,0:T(8,128)(2,1)S(1)} %bitcast.2) | data formatting | bytes 442368

commit v3 on v2

v3 whole, which is shorter than its diff:
```python
import functools

import jax
import jax.numpy as jnp
import ml_dtypes
import numpy as np
from jax import lax
from jax.experimental import pallas as pl
from jax.experimental.pallas import tpu as pltpu
from jax.sharding import PartitionSpec as P

MESH = pl.DeviceIdType.MESH
BF = jnp.bfloat16
F32 = jnp.float32
EPSILON = 1e-05
C = 192
CC = 384
ROWS, COLS = 12, 24
OWN = ROWS * COLS
UNIT = 18
WIN = 72
PAD = 80
HEAD = 32
Q_SCALE = float(HEAD**-0.5 * np.log2(np.e))
V_SCALE = 2.0**-8
FAR = -1e30
HALO = 160
LAT_AT, LON_AT, DIAG_AT = 0, 64, 128
HALO2 = 208
RESULTS = (
    (0, 4 * PAD, 32, 2),
    (16, 4 * PAD + 32, 32, 0),
    (32, 4 * PAD + 64, 32, 1),
    (PAD, 4 * PAD + 96, 48, 0),
    (2 * PAD, 4 * PAD + 144, 64, 1),
)
TOKENS = ((DIAG_AT, OWN + DIAG_AT, 32, 2), (LAT_AT, OWN + LAT_AT, 64, 0), (LON_AT, OWN + LON_AT, 64, 1))
ENCODED = ((2 * PAD, 3 * PAD, PAD, 2), (PAD, 2 * PAD, PAD, 0), (0, PAD, PAD, 1))


def one_hot(rows, cols, pairs):
    out = np.zeros((rows, cols), np.float32)
    for r, c in pairs:
        out[r, c] = 1.0
    return out.astype(ml_dtypes.bfloat16)


def halo_slot():
    for j in range(3):
        yield LAT_AT + j * UNIT, (0, j + 1)
        yield LON_AT + j * UNIT, (j + 1, 0)
    yield DIAG_AT, (0, 0)


def received(a, b):
    if a == 3 and b == 3:
        return DIAG_AT
    if a == 3:
        return LAT_AT + b * UNIT
    if b == 3:
        return LON_AT + a * UNIT
    return None


def window_row(a, b):
    return ((a // 2) * 2 + b // 2) * PAD + ((a % 2) * 2 + b % 2) * UNIT


def arrival(a, b):
    if a < 3 and b < 3:
        return window_row(a + 1, b + 1)
    which = {(3, 0): 1, (3, 1): 3, (3, 2): 3, (0, 3): 2, (1, 3): 4, (2, 3): 4, (3, 3): 0}[a, b]
    theirs = window_row(0 if a == 3 else a + 1, 0 if b == 3 else b + 1)
    return RESULTS[which][1] + theirs - RESULTS[which][0]


def natural(level, r, c):
    n = r * COLS + c
    return n if level == 0 else OWN - 1 - n


@functools.cache
def tables():
    units = [(a, b) for a in range(4) for b in range(4)]
    send1, gather1, final = [], [], []
    for level in range(2):

        def own(a, b, t, level=level):
            return natural(level, a * 3 + t // 6, b * 6 + t % 6)

        send1.append(
            one_hot(HALO, OWN, [(s + t, own(a, b, t)) for s, (a, b) in halo_slot() for t in range(UNIT)])
        )
        pairs = []
        for a, b in units:
            slot = received(a, b)
            for t in range(UNIT):
                source = own(a + 1, b + 1, t) if slot is None else OWN + slot + t
                pairs.append((window_row(a, b) + t, source))
        gather1.append(one_hot(4 * PAD, OWN + HALO, pairs))
        pairs = []
        for r in range(ROWS):
            for c in range(COLS):
                qr, qc = int(r < 6), int(c < 12)
                y, x = r % 6, c % 12
                k = y % 2 + 2 * (x % 2)
                t = (y // 2) * 6 + x // 2
                pairs.append((natural(level, r, c), (qr * 2 + qc) * PAD + k * UNIT + t))
        final.append(one_hot(OWN, 4 * PAD, pairs))
    pairs = []
    for y in range(ROWS):
        for x in range(COLS):
            a, b, t = y // 3, x // 6, (y % 3) * 6 + x % 6
            source = arrival(a, b) + t
            k = y % 2 + 2 * (x % 2)
            i, j = y // 2, x // 2
            cell = ((i // 3) * 2 + j // 6) * UNIT + (i % 3) * 6 + j % 6
            pairs.append((k * PAD + cell, source))
    gather2 = one_hot(4 * PAD, 4 * PAD + HALO2, pairs)
    pairs = []
    for quarter in range(4):
        for k in range(4):
            for t in range(UNIT):
                pairs.append((quarter * PAD + k * UNIT + t, k * PAD + quarter * UNIT + t))
    send3 = one_hot(4 * PAD, 4 * PAD, pairs)
    ones4 = np.zeros((4 * PAD, 128), np.float32)
    ones2 = np.zeros((224, 128), np.float32)
    for h in range(4):
        ones4[h * PAD : h * PAD + WIN, h * HEAD : (h + 1) * HEAD] = 1.0
    for h in range(2):
        ones2[64 + h * PAD : 64 + h * PAD + WIN, h * HEAD : (h + 1) * HEAD] = 1.0
    ones2[64 : 64 + WIN, 2 * HEAD :] = 1.0
    side_q = np.arange(PAD) >= WIN // 2
    side_k = np.arange(6 * PAD) % PAD >= WIN // 2
    far = np.where(side_q[:, None] != side_k[None, :], np.float32(FAR), np.float32(0.0))
    return dict(
        send1=np.stack(send1),
        gather1=np.stack(gather1),
        gather2=gather2,
        send3=send3,
        final=np.stack(final),
        ones4=ones4.astype(ml_dtypes.bfloat16),
        ones2=ones2.astype(ml_dtypes.bfloat16),
        far=far.astype(np.float32),
    )


ARGUMENTS = ("tokens", "norm_gain", "qkv_weight", "proj_weight", "merge_gain", "merge_weight", "coarse_gain", "coarse_qkv")
ARGUMENTS += ("coarse_proj", "up_weight", "up_gain", "out_weight")
EARLY = ("send1", "norm_gain", "qkv_weight", "far", "ones4", "ones2", "proj_weight", "gather1")
TABLES = ("send1", "gather1", "gather2", "send3", "final", "ones4", "ones2", "far")


def dot(a, b):
    return jnp.dot(a, b, preferred_element_type=F32)


def centre(values, gain):
    centred = values - jnp.mean(values, axis=-1, keepdims=True)
    spread = jnp.mean(centred * centred, axis=-1, keepdims=True)
    return (centred * gain).astype(BF), lax.rsqrt(spread + EPSILON)


def dot_t(a, b):
    return lax.dot_general(a, b, (((1,), (1,)), ((), ())), preferred_element_type=F32)


def shared(raised, values, ones):
    both = dot(raised, jnp.concatenate([values, ones], axis=1))
    return both[:, 0:128] / (both[:, 128:256] * V_SCALE)


def attend4(q, k, v, ones4, masks, far):
    keys = jnp.concatenate([k * m for m in masks], axis=0)
    raised = jnp.exp2(dot_t(q, keys) + far).astype(BF)
    small = v * jnp.bfloat16(V_SCALE)
    return shared(raised, jnp.concatenate([small * m for m in masks], axis=0), ones4)


def attend6(q, k, v, ones4, ones2, masks, far):
    zero = jnp.zeros((PAD, 128), BF)
    k0, k1 = k[:, 0:128], k[:, 128:256]
    keys = [jnp.concatenate([k0 * m, zero], axis=1) for m in masks]
    keys += [jnp.concatenate([zero, k1 * m], axis=1) for m in masks[0:2]]
    scores = dot_t(q, jnp.concatenate(keys, axis=0))
    if far is not None:
        scores = scores + far
    raised = jnp.exp2(scores).astype(BF)
    small = v * jnp.bfloat16(V_SCALE)
    v0, v1 = small[:, 0:128], small[:, 128:256]
    first = shared(raised[:, 0 : 4 * PAD], jnp.concatenate([v0 * m for m in masks], axis=0), ones4)
    last = [zero[0:64]] + [v1 * m for m in masks[0:2]]
    last = shared(raised[:, 256 : 6 * PAD], jnp.concatenate(last, axis=0), ones2)
    return jnp.concatenate([first, last], axis=1).astype(BF)


def kernel(lat_n, lon_n, *refs):
    names = list(ARGUMENTS)
    names += list(TABLES)
    hbm = dict(zip(names, refs))
    out_ref = refs[len(names)]
    scratch = refs[len(names) + 1 :]
    vm = dict(zip(names[1:], scratch))
    (qkv_pad, up_pad, far_v, buf1, buf2, buf3, snd1, snd3, load_sem, tok_sem, send_sem, recv_sem) = scratch[
        len(names) - 1 :
    ]

    lat, lon = lax.axis_index("lat"), lax.axis_index("lon")
    up, down = lax.rem(lat + 1, lat_n), lax.rem(lat + lat_n - 1, lat_n)
    east, west = lax.rem(lon + 1, lon_n), lax.rem(lon + lon_n - 1, lon_n)
    fore = ((up, lon), (lat, east), (up, east))
    back = ((down, lon), (lat, west), (down, west))

    barrier = pltpu.get_barrier_semaphore()
    for device in fore + back:
        pl.semaphore_signal(barrier, inc=1, device_id=device, device_id_type=MESH)

    loads = {}
    for level in range(2):
        loads["tokens", level] = pltpu.make_async_copy(
            hbm["tokens"].at[level], buf1.at[level, pl.ds(0, OWN)], tok_sem.at[level]
        )
        loads["tokens", level].start()
    order = ["send1"] + [n for n in EARLY if n != "send1"]
    order += [n for n in names[1:] if n not in order]

    def load(*wanted):
        for n in wanted:
            loads[n] = pltpu.make_async_copy(hbm[n], vm[n], load_sem.at[order.index(n)])
            loads[n].start()

    load("send1")

    def need(*wanted):
        for n in wanted:
            loads.pop(n).wait()

    def row(n):
        return vm[n][...].reshape(1, -1)

    def send(stage, level, which, source, target, plan):
        forward = (level == 1) if stage < 2 else (level == 0)
        copies = {}
        for i in which:
            start, place, rows, neighbour = plan[i]
            copies[i] = pltpu.make_async_remote_copy(
                src_ref=source.at[level, pl.ds(start, rows)],
                dst_ref=target.at[level, pl.ds(place, rows)],
                send_sem=send_sem.at[stage, level, i],
                recv_sem=recv_sem.at[stage, level, i],
                device_id=(fore if forward else back)[neighbour],
                device_id_type=MESH,
            )
            copies[i].start()
        return copies

    need("send1")
    for level in range(2):
        need(("tokens", level))
        snd1[level] = dot(vm["send1"][level], buf1[level, 0:OWN]).astype(BF)
    pl.semaphore_wait(barrier, 6)
    one = [send(0, level, (0, 1, 2), snd1, buf1, TOKENS) for level in range(2)]
    load(*order[1:])

    need("qkv_weight", "far")
    zero = jnp.zeros((C, 64), BF)
    for part in range(3):
        qkv_pad[:, part * 256 : part * 256 + C] = vm["qkv_weight"][:, part * C : (part + 1) * C]
        qkv_pad[:, part * 256 + C : (part + 1) * 256] = zero
    edge = (lat_n - 1, 0)
    for level in range(2):
        far_v[level] = jnp.where(lat == edge[level], vm["far"][...], 0.0)
    need("norm_gain", "ones4", "ones2", "proj_weight", "gather1")
    lane = lax.broadcasted_iota(jnp.int32, (PAD, 128), 1)
    masks = [jnp.where(lane // HEAD == h, 1.0, 0.0).astype(BF) for h in range(4)]
    ones4, ones2 = vm["ones4"], vm["ones2"]

    def fine(tokens, items):
        normed, scale = centre(tokens, row("norm_gain"))
        packed = dot(normed, qkv_pad[...]) * scale
        q = (packed[:, 0:256] * Q_SCALE).astype(BF)
        k = packed[:, 256:512].astype(BF)
        v = packed[:, 512:768].astype(BF)
        heads = []
        for i, (level, w) in enumerate(items):
            at = slice(i * PAD, (i + 1) * PAD)
            far = far_v[level] if w >= 2 else None
            heads.append(attend6(q[at], k[at], v[at], ones4[...], ones2[...], masks, far))
        heads = jnp.concatenate(heads, axis=0)[:, 0:C]
        result = (tokens + dot(heads, vm["proj_weight"][...])).astype(BF)
        for i, (level, w) in enumerate(items):
            buf2[level, w * PAD : (w + 1) * PAD] = result[i * PAD : (i + 1) * PAD]

    first = [dot(vm["gather1"][level, 0:PAD, 0:OWN], buf1[level, 0:OWN]) for level in range(2)]
    fine(jnp.concatenate(first, axis=0), [(0, 0), (1, 0)])

    two = [send(1, level, (0, 1, 2), buf2, buf2, RESULTS) for level in range(2)]

    for level in range(2):
        one[level][1].wait_recv()
        one[level][2].wait_recv()
    near = OWN + DIAG_AT
    rest = [dot(vm["gather1"][level, PAD : 3 * PAD, 0:near], buf1[level, 0:near]) for level in range(2)]
    fine(jnp.concatenate(rest, axis=0), [(0, 1), (0, 2), (1, 1), (1, 2)])
    for level in range(2):
        two[level].update(send(1, level, (3, 4), buf2, buf2, RESULTS))
    for level in range(2):
        one[level][0].wait_recv()
    last = [dot(vm["gather1"][level, 3 * PAD : 4 * PAD], buf1[level]) for level in range(2)]
    fine(jnp.concatenate(last, axis=0), [(0, 3), (1, 3)])

    need("up_weight")
    for k in range(4):
        up_pad[:, k * 256 : k * 256 + C] = vm["up_weight"][:, k * C : (k + 1) * C]
    need("gather2", "send3", "merge_gain", "merge_weight", "coarse_gain", "coarse_qkv", "coarse_proj")
    need("up_gain", "out_weight", "final")

    for level in range(2):
        for copy in two[level].values():
            copy.wait_recv()
    cells = [dot(vm["gather2"][...], buf2[level]) for level in range(2)]
    group = [
        jnp.concatenate([cells[0][k * PAD : (k + 1) * PAD], cells[1][(3 - k) * PAD : (4 - k) * PAD]], axis=0)
        for k in range(4)
    ]
    average = jnp.sum(group[0] + group[1] + group[2] + group[3], axis=-1, keepdims=True) * (1.0 / (4 * C))
    centred = [g - average for g in group]
    squares = [c * c for c in centred]
    spread = jnp.sum(squares[0] + squares[1] + squares[2] + squares[3], axis=-1, keepdims=True) * (1.0 / (4 * C))
    scale = lax.rsqrt(spread + EPSILON)
    coarse = jnp.zeros((2 * PAD, CC), F32)
    for k in range(4):
        stacked = (centred[k] * row("merge_gain")[:, k * C : (k + 1) * C]).astype(BF)
        coarse = coarse + dot(stacked, vm["merge_weight"][k * C : (k + 1) * C])
    coarse = (coarse * scale).astype(BF).astype(F32)
    normed, scale = centre(coarse, row("coarse_gain"))
    packed = dot(normed, vm["coarse_qkv"][...]) * scale
    q = (packed[:, 0:CC] * Q_SCALE).astype(BF)
    k = packed[:, CC : 2 * CC].astype(BF)
    v = packed[:, 2 * CC : 3 * CC].astype(BF)
    heads = []
    for level in range(2):
        at = slice(level * PAD, (level + 1) * PAD)
        parts = []
        for j in range(3):
            cut = slice(j * 128, (j + 1) * 128)
            far = far_v[level, :, 0 : 4 * PAD]
            parts.append(attend4(q[at, cut], k[at, cut], v[at, cut], ones4[...], masks, far).astype(BF))
        heads.append(jnp.concatenate(parts, axis=1))
    heads = jnp.concatenate(heads, axis=0)
    coarse_out = (coarse + dot(heads, vm["coarse_proj"][...])).astype(BF)
    lifted = [dot(coarse_out, up_pad[:, k * 256 : k * 256 + C]) for k in range(4)]
    normed = [centre(x, row("up_gain")) for x in lifted]
    branch = dot(jnp.concatenate([n for n, _ in normed], axis=0), vm["out_weight"][...])
    encoded = [(group[k] + branch[k * 2 * PAD : (k + 1) * 2 * PAD] * normed[k][1]).astype(BF) for k in range(4)]
    three = []
    for level in range(2):
        order = range(4) if level == 0 else range(3, -1, -1)
        mine = jnp.concatenate([encoded[k][level * PAD : (level + 1) * PAD] for k in order], axis=0)
        quarters = dot(vm["send3"][...], mine).astype(BF)
        buf3[level, 0:PAD] = quarters[0:PAD]
        snd3[level] = quarters[PAD : 4 * PAD]
        three.append(send(2, level, (0, 1, 2), snd3, buf3, ENCODED))

    for level in range(2):
        for copy in three[level].values():
            copy.wait_recv()
        out_ref[level] = dot(vm["final"][level], buf3[level]).astype(BF)
    for copies in one + two + three:
        for copy in copies.values():
            copy.wait_send()


def body(lat_n, lon_n, tokens, norm_gain, qkv_weight, proj_weight, merge_gain, merge_weight, coarse_gain, *rest):
    coarse_qkv, coarse_proj, up_weight, up_gain, out_weight = rest
    table = tables()
    args = [
        tokens.reshape(2, OWN, C),
        norm_gain,
        qkv_weight,
        proj_weight,
        merge_gain,
        merge_weight,
        coarse_gain,
        coarse_qkv,
        coarse_proj,
        up_weight,
        up_gain,
        out_weight,
    ] + [jnp.asarray(table[n]) for n in TABLES]
    scratch = [pltpu.VMEM(a.shape, a.dtype) for a in args[1:]]
    scratch += [
        pltpu.VMEM((C, 768), BF),
        pltpu.VMEM((CC, 1024), BF),
        pltpu.VMEM((2, PAD, 6 * PAD), F32),
        pltpu.VMEM((2, OWN + HALO, C), BF),
        pltpu.VMEM((2, 4 * PAD + HALO2, C), BF),
        pltpu.VMEM((2, 4 * PAD, C), BF),
        pltpu.VMEM((2, HALO, C), BF),
        pltpu.VMEM((2, 3 * PAD, C), BF),
        pltpu.SemaphoreType.DMA((len(args) - 1,)),
        pltpu.SemaphoreType.DMA((2,)),
        pltpu.SemaphoreType.DMA((3, 2, 5)),
        pltpu.SemaphoreType.DMA((3, 2, 5)),
    ]
    out = pl.pallas_call(
        functools.partial(kernel, lat_n, lon_n),
        out_shape=jax.ShapeDtypeStruct((2, OWN, C), BF),
        in_specs=[pl.BlockSpec(memory_space=pltpu.HBM)] * len(args),
        out_specs=pl.BlockSpec(memory_space=pltpu.VMEM),
        scratch_shapes=scratch,
        compiler_params=pltpu.CompilerParams(
            collective_id=0, has_side_effects=True, vmem_limit_bytes=40 * 1024 * 1024
        ),
    )(*[pltpu.with_memory_space_constraint(a, pltpu.HBM) for a in args])
    return out.reshape(tokens.shape)


def solution(mesh):
    placed = (P(None, "lat", "lon", None),) + (P(),) * 11
    return jax.shard_map(
        functools.partial(body, mesh.shape["lat"], mesh.shape["lon"]),
        mesh=mesh,
        in_specs=placed,
        out_specs=P(None, "lat", "lon", None),
        check_vma=False,
    )
```

time: 35.9 us -> 34.3 us (0.955)
  the two profiles are of different devices: /device:TPU:24 before, /device:TPU:1 now
where the time goes in v3:
time: 34.3 us; the launch traced here: 34.2 us
  Pallas kernels  33.5 us (98%)
  local copies, waits for them, and re-layouts  0.72 us (2%)
    pallas_call x1, Pallas kernels, body(): pl.pallas_call(functools.partial(kernel, lat_n, lon_n), out_shape=jax.Sha...  33.5 us
    unnamed x1, local copies, waits for them, and re-layouts  0.72 us

profile of v3, /device:TPU:1, one launch (start us, length us, event | category | flops | bytes accessed | tf_op | source)
XLA Modules:
  0.0 34.2 jit_solution(3971414486813667969)
XLA Ops:
  0.0 33.5 %shard_map.190 = bf16[2,288,192]{2,1,0:T(8,128)(2,1)S(1)} custom-call(bf16[2,288,192]{2,1,0:T(8,128)(2,1)} %bitcast.3, f32[192]{0:T(256)} %refs_1_.1, bf16[192,576]{1,0:T(8,128)(2,1)} %refs_2_.1, bf16[192,192]{1,0:T(8,128)(2,1)} %refs_3_.1, f32[768]{0:T(1024)} %refs_4_.1, bf16[768,384]{1,0:T(8,128)(2,1)} %refs_5_.1, f32[384]{0:T(512)} %refs_6_.1, ...), custom_call_target="tpu_custom_call" | custom-call | tf_op jit(solution)/shard_map/pallas_call | solution.py:406
  33.5 0.7 %copy.22 = bf16[2,12,24,192]{3,2,1,0:T(8,128)(2,1)} copy(bf16[2,12,24,192]{3,2,1,0:T(8,128)(2,1)S(1)} %bitcast.2) | data formatting | bytes 442368

commit v4 on v3

--- a/solution.py
+++ b/solution.py
@@ -27,6 +27,7 @@
 HALO = 160
 LAT_AT, LON_AT, DIAG_AT = 0, 64, 128
 HALO2 = 208
+MIRROR = (2, 3)
 RESULTS = (
     (0, 4 * PAD, 32, 2),
     (16, 4 * PAD + 32, 32, 0),
@@ -75,8 +76,7 @@
 
 
 def natural(level, r, c):
-    n = r * COLS + c
-    return n if level == 0 else OWN - 1 - n
+    return (r if level == 0 else ROWS - 1 - r) * COLS + COLS - 1 - c
 
 
 @functools.cache
@@ -208,11 +208,11 @@
     lat, lon = lax.axis_index("lat"), lax.axis_index("lon")
     up, down = lax.rem(lat + 1, lat_n), lax.rem(lat + lat_n - 1, lat_n)
     east, west = lax.rem(lon + 1, lon_n), lax.rem(lon + lon_n - 1, lon_n)
-    fore = ((up, lon), (lat, east), (up, east))
-    back = ((down, lon), (lat, west), (down, west))
+    takers = (((down, lon), (lat, east), (down, east)), ((up, lon), (lat, east), (up, east)))
+    owners = (((up, lon), (lat, west), (up, west)), ((down, lon), (lat, west), (down, west)))
 
     barrier = pltpu.get_barrier_semaphore()
-    for device in fore + back:
+    for device in ((up, lon), (down, lon), (lat, east), (lat, west)) + tuple((a, b) for a in (up, down) for b in (east, west)):
         pl.semaphore_signal(barrier, inc=1, device_id=device, device_id_type=MESH)
 
     loads = {}
@@ -239,7 +239,7 @@
         return vm[n][...].reshape(1, -1)
 
     def send(stage, level, which, source, target, plan):
-        forward = (level == 1) if stage < 2 else (level == 0)
+        devices = (takers if stage < 2 else owners)[level]
         copies = {}
         for i in which:
             start, place, rows, neighbour = plan[i]
@@ -248,7 +248,7 @@
                 dst_ref=target.at[level, pl.ds(place, rows)],
                 send_sem=send_sem.at[stage, level, i],
                 recv_sem=recv_sem.at[stage, level, i],
-                device_id=(fore if forward else back)[neighbour],
+                device_id=devices[neighbour],
                 device_id_type=MESH,
             )
             copies[i].start()
@@ -258,7 +258,7 @@
     for level in range(2):
         need(("tokens", level))
         snd1[level] = dot(vm["send1"][level], buf1[level, 0:OWN]).astype(BF)
-    pl.semaphore_wait(barrier, 6)
+    pl.semaphore_wait(barrier, 8)
     one = [send(0, level, (0, 1, 2), snd1, buf1, TOKENS) for level in range(2)]
     load(*order[1:])
 
@@ -296,14 +296,20 @@
 
     two = [send(1, level, (0, 1, 2), buf2, buf2, RESULTS) for level in range(2)]
 
+    near = OWN + LON_AT
     for level in range(2):
         one[level][1].wait_recv()
+    rest = [dot(vm["gather1"][level, 2 * PAD : 3 * PAD, 0:near], buf1[level, 0:near]) for level in range(2)]
+    fine(jnp.concatenate(rest, axis=0), [(0, 2), (1, 2)])
+    for level in range(2):
+        two[level].update(send(1, level, (4,), buf2, buf2, RESULTS))
+    near = OWN + DIAG_AT
+    for level in range(2):
         one[level][2].wait_recv()
-    near = OWN + DIAG_AT
-    rest = [dot(vm["gather1"][level, PAD : 3 * PAD, 0:near], buf1[level, 0:near]) for level in range(2)]
-    fine(jnp.concatenate(rest, axis=0), [(0, 1), (0, 2), (1, 1), (1, 2)])
-    for level in range(2):
-        two[level].update(send(1, level, (3, 4), buf2, buf2, RESULTS))
+    rest = [dot(vm["gather1"][level, PAD : 2 * PAD, 0:near], buf1[level, 0:near]) for level in range(2)]
+    fine(jnp.concatenate(rest, axis=0), [(0, 1), (1, 1)])
+    for level in range(2):
+        two[level].update(send(1, level, (3,), buf2, buf2, RESULTS))
     for level in range(2):
         one[level][0].wait_recv()
     last = [dot(vm["gather1"][level, 3 * PAD : 4 * PAD], buf1[level]) for level in range(2)]
@@ -320,7 +326,7 @@
             copy.wait_recv()
     cells = [dot(vm["gather2"][...], buf2[level]) for level in range(2)]
     group = [
-        jnp.concatenate([cells[0][k * PAD : (k + 1) * PAD], cells[1][(3 - k) * PAD : (4 - k) * PAD]], axis=0)
+        jnp.concatenate([cells[level][(k ^ m) * PAD : ((k ^ m) + 1) * PAD] for level, m in enumerate(MIRROR)], axis=0)
         for k in range(4)
     ]
     average = jnp.sum(group[0] + group[1] + group[2] + group[3], axis=-1, keepdims=True) * (1.0 / (4 * C))
@@ -355,8 +361,8 @@
     encoded = [(group[k] + branch[k * 2 * PAD : (k + 1) * 2 * PAD] * normed[k][1]).astype(BF) for k in range(4)]
     three = []
     for level in range(2):
-        order = range(4) if level == 0 else range(3, -1, -1)
-        mine = jnp.concatenate([encoded[k][level * PAD : (level + 1) * PAD] for k in order], axis=0)
+        mine = [encoded[k ^ MIRROR[level]][level * PAD : (level + 1) * PAD] for k in range(4)]
+        mine = jnp.concatenate(mine, axis=0)
         quarters = dot(vm["send3"][...], mine).astype(BF)
         buf3[level, 0:PAD] = quarters[0:PAD]
         snd3[level] = quarters[PAD : 4 * PAD]

time: 34.3 us -> 33.7 us (0.983)
  the two profiles are of different devices: /device:TPU:1 before, /device:TPU:2 now
where the time goes in v4:
time: 33.7 us; the launch traced here: 33.6 us
  Pallas kernels  32.8 us (97%)
  local copies, waits for them, and re-layouts  0.72 us (2%)
    pallas_call x1, Pallas kernels, body(): pl.pallas_call(functools.partial(kernel, lat_n, lon_n), out_shape=jax.Sha...  32.8 us
    unnamed x1, local copies, waits for them, and re-layouts  0.72 us

profile of v4, /device:TPU:2, one launch (start us, length us, event | category | flops | bytes accessed | tf_op | source)
XLA Modules:
  0.0 33.6 jit_solution(13001929449119683044)
XLA Ops:
  0.0 32.8 %shard_map.190 = bf16[2,288,192]{2,1,0:T(8,128)(2,1)S(1)} custom-call(bf16[2,288,192]{2,1,0:T(8,128)(2,1)} %bitcast.3, f32[192]{0:T(256)} %refs_1_.1, bf16[192,576]{1,0:T(8,128)(2,1)} %refs_2_.1, bf16[192,192]{1,0:T(8,128)(2,1)} %refs_3_.1, f32[768]{0:T(1024)} %refs_4_.1, bf16[768,384]{1,0:T(8,128)(2,1)} %refs_5_.1, f32[384]{0:T(512)} %refs_6_.1, ...), custom_call_target="tpu_custom_call" | custom-call | tf_op jit(solution)/shard_map/pallas_call | solution.py:412
  32.8 0.7 %copy.22 = bf16[2,12,24,192]{3,2,1,0:T(8,128)(2,1)} copy(bf16[2,12,24,192]{3,2,1,0:T(8,128)(2,1)S(1)} %bitcast.2) | data formatting | bytes 442368

commit v5 on v4

--- a/solution.py
+++ b/solution.py
@@ -26,16 +26,16 @@
 FAR = -1e30
 HALO = 160
 LAT_AT, LON_AT, DIAG_AT = 0, 64, 128
-HALO2 = 208
+HALO2 = 192
 MIRROR = (2, 3)
 RESULTS = (
     (0, 4 * PAD, 32, 2),
     (16, 4 * PAD + 32, 32, 0),
     (32, 4 * PAD + 64, 32, 1),
     (PAD, 4 * PAD + 96, 48, 0),
-    (2 * PAD, 4 * PAD + 144, 64, 1),
+    (2 * PAD, 4 * PAD + 144, 48, 1),
 )
-TOKENS = ((DIAG_AT, OWN + DIAG_AT, 32, 2), (LAT_AT, OWN + LAT_AT, 64, 0), (LON_AT, OWN + LON_AT, 64, 1))
+TOKENS = ((LON_AT, OWN + LON_AT, 64, 1), (LAT_AT, OWN + LAT_AT, 64, 0), (DIAG_AT, OWN + DIAG_AT, 32, 2))
 ENCODED = ((2 * PAD, 3 * PAD, PAD, 2), (PAD, 2 * PAD, PAD, 0), (0, PAD, PAD, 1))
 
 
@@ -64,7 +64,10 @@
 
 
 def window_row(a, b):
-    return ((a // 2) * 2 + b // 2) * PAD + ((a % 2) * 2 + b % 2) * UNIT
+    window, inner = (a // 2) * 2 + b // 2, (a % 2) * 2 + b % 2
+    if window == 2:
+        inner = (b % 2) * 2 + a % 2
+    return window * PAD + inner * UNIT
 
 
 def arrival(a, b):
@@ -130,9 +133,12 @@
     for h in range(2):
         ones2[64 + h * PAD : 64 + h * PAD + WIN, h * HEAD : (h + 1) * HEAD] = 1.0
     ones2[64 : 64 + WIN, 2 * HEAD :] = 1.0
-    side_q = np.arange(PAD) >= WIN // 2
-    side_k = np.arange(6 * PAD) % PAD >= WIN // 2
-    far = np.where(side_q[:, None] != side_k[None, :], np.float32(FAR), np.float32(0.0))
+    far = []
+    for by_column in (False, True):
+        units_of = np.arange(PAD) // UNIT
+        side = (units_of % 2 if by_column else units_of // 2) == 1
+        far.append(np.where(side[:, None] != np.tile(side, 6)[None, :], np.float32(FAR), np.float32(0.0)))
+    far = np.stack(far)
     return dict(
         send1=np.stack(send1),
         gather1=np.stack(gather1),
@@ -141,7 +147,7 @@
         final=np.stack(final),
         ones4=ones4.astype(ml_dtypes.bfloat16),
         ones2=ones2.astype(ml_dtypes.bfloat16),
-        far=far.astype(np.float32),
+        far=far.astype(ml_dtypes.bfloat16),
     )
 
 
@@ -229,7 +235,7 @@
             loads[n] = pltpu.make_async_copy(hbm[n], vm[n], load_sem.at[order.index(n)])
             loads[n].start()
 
-    load("send1")
+    load(*order[:len(EARLY)])
 
     def need(*wanted):
         for n in wanted:
@@ -259,8 +265,11 @@
         need(("tokens", level))
         snd1[level] = dot(vm["send1"][level], buf1[level, 0:OWN]).astype(BF)
     pl.semaphore_wait(barrier, 8)
-    one = [send(0, level, (0, 1, 2), snd1, buf1, TOKENS) for level in range(2)]
-    load(*order[1:])
+    one = [{}, {}]
+    for i in range(3):
+        for level in range(2):
+            one[level].update(send(0, level, (i,), snd1, buf1, TOKENS))
+    load(*order[len(EARLY):])
 
     need("qkv_weight", "far")
     zero = jnp.zeros((C, 64), BF)
@@ -269,7 +278,7 @@
         qkv_pad[:, part * 256 + C : (part + 1) * 256] = zero
     edge = (lat_n - 1, 0)
     for level in range(2):
-        far_v[level] = jnp.where(lat == edge[level], vm["far"][...], 0.0)
+        far_v[level] = jnp.where(lat == edge[level], vm["far"][...].astype(F32), 0.0)
     need("norm_gain", "ones4", "ones2", "proj_weight", "gather1")
     lane = lax.broadcasted_iota(jnp.int32, (PAD, 128), 1)
     masks = [jnp.where(lane // HEAD == h, 1.0, 0.0).astype(BF) for h in range(4)]
@@ -284,7 +293,7 @@
         heads = []
         for i, (level, w) in enumerate(items):
             at = slice(i * PAD, (i + 1) * PAD)
-            far = far_v[level] if w >= 2 else None
+            far = far_v[level, 3 - w] if w >= 2 else None
             heads.append(attend6(q[at], k[at], v[at], ones4[...], ones2[...], masks, far))
         heads = jnp.concatenate(heads, axis=0)[:, 0:C]
         result = (tokens + dot(heads, vm["proj_weight"][...])).astype(BF)
@@ -305,13 +314,13 @@
         two[level].update(send(1, level, (4,), buf2, buf2, RESULTS))
     near = OWN + DIAG_AT
     for level in range(2):
-        one[level][2].wait_recv()
+        one[level][0].wait_recv()
     rest = [dot(vm["gather1"][level, PAD : 2 * PAD, 0:near], buf1[level, 0:near]) for level in range(2)]
     fine(jnp.concatenate(rest, axis=0), [(0, 1), (1, 1)])
     for level in range(2):
         two[level].update(send(1, level, (3,), buf2, buf2, RESULTS))
     for level in range(2):
-        one[level][0].wait_recv()
+        one[level][2].wait_recv()
     last = [dot(vm["gather1"][level, 3 * PAD : 4 * PAD], buf1[level]) for level in range(2)]
     fine(jnp.concatenate(last, axis=0), [(0, 3), (1, 3)])
 
@@ -350,7 +359,7 @@
         parts = []
         for j in range(3):
             cut = slice(j * 128, (j + 1) * 128)
-            far = far_v[level, :, 0 : 4 * PAD]
+            far = far_v[level, 0, :, 0 : 4 * PAD]
             parts.append(attend4(q[at, cut], k[at, cut], v[at, cut], ones4[...], masks, far).astype(BF))
         heads.append(jnp.concatenate(parts, axis=1))
     heads = jnp.concatenate(heads, axis=0)
@@ -398,7 +407,7 @@
     scratch += [
         pltpu.VMEM((C, 768), BF),
         pltpu.VMEM((CC, 1024), BF),
-        pltpu.VMEM((2, PAD, 6 * PAD), F32),
+        pltpu.VMEM((2, 2, PAD, 6 * PAD), F32),
         pltpu.VMEM((2, OWN + HALO, C), BF),
         pltpu.VMEM((2, 4 * PAD + HALO2, C), BF),
         pltpu.VMEM((2, 4 * PAD, C), BF),

time: 33.7 us -> 33.2 us (0.985)
  Pallas kernels: 32.8 us -> 32.3 us
    pallas_call x1, Pallas kernels: 32.8 us -> 32.3 us  [body(): pl.pallas_call(functools.partial(kernel, lat_n, lon_n), out_shape=jax.Sha...]
where the time goes in v5:
time: 33.2 us; the launch traced here: 33 us
  Pallas kernels  32.3 us (97%)
  local copies, waits for them, and re-layouts  0.72 us (2%)
    pallas_call x1, Pallas kernels, body(): pl.pallas_call(functools.partial(kernel, lat_n, lon_n), out_shape=jax.Sha...  32.3 us
    unnamed x1, local copies, waits for them, and re-layouts  0.72 us

profile of v5, /device:TPU:2, one launch (start us, length us, event | category | flops | bytes accessed | tf_op | source)
XLA Modules:
  0.0 33.0 jit_solution(2373076159079013407)
XLA Ops:
  0.0 32.3 %shard_map.190 = bf16[2,288,192]{2,1,0:T(8,128)(2,1)S(1)} custom-call(bf16[2,288,192]{2,1,0:T(8,128)(2,1)} %bitcast.3, f32[192]{0:T(256)} %refs_1_.1, bf16[192,576]{1,0:T(8,128)(2,1)} %refs_2_.1, bf16[192,192]{1,0:T(8,128)(2,1)} %refs_3_.1, f32[768]{0:T(1024)} %refs_4_.1, bf16[768,384]{1,0:T(8,128)(2,1)} %refs_5_.1, f32[384]{0:T(512)} %refs_6_.1, ...), custom_call_target="tpu_custom_call" | custom-call | tf_op jit(solution)/shard_map/pallas_call | solution.py:421
  32.3 0.7 %copy.22 = bf16[2,12,24,192]{3,2,1,0:T(8,128)(2,1)} copy(bf16[2,12,24,192]{3,2,1,0:T(8,128)(2,1)S(1)} %bitcast.2) | data formatting | bytes 442368

commit v6 on v5

--- a/solution.py
+++ b/solution.py
@@ -305,6 +305,16 @@
 
     two = [send(1, level, (0, 1, 2), buf2, buf2, RESULTS) for level in range(2)]
 
+    for level in range(2):
+        one[level][0].wait_recv()
+    rest = []
+    for level in range(2):
+        own = dot(vm["gather1"][level, PAD : 2 * PAD, 0:OWN], buf1[level, 0:OWN])
+        table = vm["gather1"][level, PAD : 2 * PAD, OWN : OWN + DIAG_AT]
+        rest.append(own + dot(table[:, LON_AT:DIAG_AT], buf1[level, OWN + LON_AT : OWN + DIAG_AT]))
+    fine(jnp.concatenate(rest, axis=0), [(0, 1), (1, 1)])
+    for level in range(2):
+        two[level].update(send(1, level, (3,), buf2, buf2, RESULTS))
     near = OWN + LON_AT
     for level in range(2):
         one[level][1].wait_recv()
@@ -312,13 +322,6 @@
     fine(jnp.concatenate(rest, axis=0), [(0, 2), (1, 2)])
     for level in range(2):
         two[level].update(send(1, level, (4,), buf2, buf2, RESULTS))
-    near = OWN + DIAG_AT
-    for level in range(2):
-        one[level][0].wait_recv()
-    rest = [dot(vm["gather1"][level, PAD : 2 * PAD, 0:near], buf1[level, 0:near]) for level in range(2)]
-    fine(jnp.concatenate(rest, axis=0), [(0, 1), (1, 1)])
-    for level in range(2):
-        two[level].update(send(1, level, (3,), buf2, buf2, RESULTS))
     for level in range(2):
         one[level][2].wait_recv()
     last = [dot(vm["gather1"][level, 3 * PAD : 4 * PAD], buf1[level]) for level in range(2)]
@@ -368,14 +371,15 @@
     normed = [centre(x, row("up_gain")) for x in lifted]
     branch = dot(jnp.concatenate([n for n, _ in normed], axis=0), vm["out_weight"][...])
     encoded = [(group[k] + branch[k * 2 * PAD : (k + 1) * 2 * PAD] * normed[k][1]).astype(BF) for k in range(4)]
-    three = []
+    three, mines = [], []
     for level in range(2):
         mine = [encoded[k ^ MIRROR[level]][level * PAD : (level + 1) * PAD] for k in range(4)]
         mine = jnp.concatenate(mine, axis=0)
-        quarters = dot(vm["send3"][...], mine).astype(BF)
-        buf3[level, 0:PAD] = quarters[0:PAD]
-        snd3[level] = quarters[PAD : 4 * PAD]
+        snd3[level] = dot(vm["send3"][PAD : 4 * PAD], mine).astype(BF)
         three.append(send(2, level, (0, 1, 2), snd3, buf3, ENCODED))
+        mines.append(mine)
+    for level in range(2):
+        buf3[level, 0:PAD] = dot(vm["send3"][0:PAD], mines[level]).astype(BF)
 
     for level in range(2):
         for copy in three[level].values():

time: 33.2 us -> 31.4 us (0.946)
  Pallas kernels: 32.3 us -> 30.5 us
    pallas_call x1, Pallas kernels: 32.3 us -> 30.5 us  [body(): pl.pallas_call(functools.partial(kernel, lat_n, lon_n), out_shape=jax.Sha...]
where the time goes in v6:
time: 31.4 us; the launch traced here: 31.3 us
  Pallas kernels  30.5 us (97%)
  local copies, waits for them, and re-layouts  0.72 us (2%)
    pallas_call x1, Pallas kernels, body(): pl.pallas_call(functools.partial(kernel, lat_n, lon_n), out_shape=jax.Sha...  30.5 us
    unnamed x1, local copies, waits for them, and re-layouts  0.72 us

profile of v6, /device:TPU:2, one launch (start us, length us, event | category | flops | bytes accessed | tf_op | source)
XLA Modules:
  0.0 31.3 jit_solution(18071217548378116305)
XLA Ops:
  0.0 30.5 %shard_map.190 = bf16[2,288,192]{2,1,0:T(8,128)(2,1)S(1)} custom-call(bf16[2,288,192]{2,1,0:T(8,128)(2,1)} %bitcast.3, f32[192]{0:T(256)} %refs_1_.1, bf16[192,576]{1,0:T(8,128)(2,1)} %refs_2_.1, bf16[192,192]{1,0:T(8,128)(2,1)} %refs_3_.1, f32[768]{0:T(1024)} %refs_4_.1, bf16[768,384]{1,0:T(8,128)(2,1)} %refs_5_.1, f32[384]{0:T(512)} %refs_6_.1, ...), custom_call_target="tpu_custom_call" | custom-call | tf_op jit(solution)/shard_map/pallas_call | solution.py:425
  30.6 0.7 %copy.22 = bf16[2,12,24,192]{3,2,1,0:T(8,128)(2,1)} copy(bf16[2,12,24,192]{3,2,1,0:T(8,128)(2,1)S(1)} %bitcast.2) | data formatting | bytes 442368

commit v7 on v6

--- a/solution.py
+++ b/solution.py
@@ -24,19 +24,25 @@
 Q_SCALE = float(HEAD**-0.5 * np.log2(np.e))
 V_SCALE = 2.0**-8
 FAR = -1e30
-HALO = 160
-LAT_AT, LON_AT, DIAG_AT = 0, 64, 128
+HALO = 176
+LAT_AT, LON_AT, LON_LAST, DIAG_AT = 0, 64, 112, 144
 HALO2 = 192
 MIRROR = (2, 3)
+SOON = 4 * PAD + 144
 RESULTS = (
     (0, 4 * PAD, 32, 2),
     (16, 4 * PAD + 32, 32, 0),
     (32, 4 * PAD + 64, 32, 1),
-    (PAD, 4 * PAD + 96, 48, 0),
-    (2 * PAD, 4 * PAD + 144, 48, 1),
+    (PAD, 4 * PAD + 144, 48, 0),
+    (2 * PAD, 4 * PAD + 96, 48, 1),
 )
-TOKENS = ((LON_AT, OWN + LON_AT, 64, 1), (LAT_AT, OWN + LAT_AT, 64, 0), (DIAG_AT, OWN + DIAG_AT, 32, 2))
-ENCODED = ((2 * PAD, 3 * PAD, PAD, 2), (PAD, 2 * PAD, PAD, 0), (0, PAD, PAD, 1))
+TOKENS = (
+    (LON_AT, OWN + LON_AT, 48, 1),
+    (LAT_AT, OWN + LAT_AT, 64, 0),
+    (DIAG_AT, OWN + DIAG_AT, 32, 2),
+    (LON_LAST, OWN + LON_LAST, 32, 1),
+)
+ENCODED = ((2 * PAD, 2 * PAD, PAD, 2), (PAD, PAD, PAD, 0), (0, 0, PAD, 1))
 
 
 def one_hot(rows, cols, pairs):
@@ -49,7 +55,7 @@
 def halo_slot():
     for j in range(3):
         yield LAT_AT + j * UNIT, (0, j + 1)
-        yield LON_AT + j * UNIT, (j + 1, 0)
+        yield (LON_LAST if j == 2 else LON_AT + j * UNIT), (j + 1, 0)
     yield DIAG_AT, (0, 0)
 
 
@@ -59,7 +65,7 @@
     if a == 3:
         return LAT_AT + b * UNIT
     if b == 3:
-        return LON_AT + a * UNIT
+        return LON_LAST if a == 2 else LON_AT + a * UNIT
     return None
 
 
@@ -142,9 +148,12 @@
     return dict(
         send1=np.stack(send1),
         gather1=np.stack(gather1),
-        gather2=gather2,
+        gather2=gather2[:, 0:SOON],
+        gather2b=gather2[:, SOON:],
+        lon1=np.stack(gather1)[:, PAD : 2 * PAD, OWN + LON_AT : OWN + LON_LAST],
         send3=send3,
-        final=np.stack(final),
+        final=np.stack(final)[:, :, 0:PAD],
+        final_b=np.stack(final)[:, :, PAD:],
         ones4=ones4.astype(ml_dtypes.bfloat16),
         ones2=ones2.astype(ml_dtypes.bfloat16),
         far=far.astype(ml_dtypes.bfloat16),
@@ -153,8 +162,8 @@
 
 ARGUMENTS = ("tokens", "norm_gain", "qkv_weight", "proj_weight", "merge_gain", "merge_weight", "coarse_gain", "coarse_qkv")
 ARGUMENTS += ("coarse_proj", "up_weight", "up_gain", "out_weight")
-EARLY = ("send1", "norm_gain", "qkv_weight", "far", "ones4", "ones2", "proj_weight", "gather1")
-TABLES = ("send1", "gather1", "gather2", "send3", "final", "ones4", "ones2", "far")
+EARLY = ("send1", "norm_gain", "qkv_weight", "far", "ones4", "ones2", "proj_weight", "gather1", "lon1")
+TABLES = ("send1", "gather1", "gather2", "gather2b", "lon1", "send3", "final", "final_b", "ones4", "ones2", "far")
 
 
 def dot(a, b):
@@ -266,7 +275,7 @@
         snd1[level] = dot(vm["send1"][level], buf1[level, 0:OWN]).astype(BF)
     pl.semaphore_wait(barrier, 8)
     one = [{}, {}]
-    for i in range(3):
+    for i in (0, 1, 3, 2):
         for level in range(2):
             one[level].update(send(0, level, (i,), snd1, buf1, TOKENS))
     load(*order[len(EARLY):])
@@ -279,7 +288,7 @@
     edge = (lat_n - 1, 0)
     for level in range(2):
         far_v[level] = jnp.where(lat == edge[level], vm["far"][...].astype(F32), 0.0)
-    need("norm_gain", "ones4", "ones2", "proj_weight", "gather1")
+    need("norm_gain", "ones4", "ones2", "proj_weight", "gather1", "lon1")
     lane = lax.broadcasted_iota(jnp.int32, (PAD, 128), 1)
     masks = [jnp.where(lane // HEAD == h, 1.0, 0.0).astype(BF) for h in range(4)]
     ones4, ones2 = vm["ones4"], vm["ones2"]
@@ -305,13 +314,11 @@
 
     two = [send(1, level, (0, 1, 2), buf2, buf2, RESULTS) for level in range(2)]
 
+    own = [dot(vm["gather1"][level, PAD : 2 * PAD, 0:OWN], buf1[level, 0:OWN]) for level in range(2)]
     for level in range(2):
         one[level][0].wait_recv()
-    rest = []
-    for level in range(2):
-        own = dot(vm["gather1"][level, PAD : 2 * PAD, 0:OWN], buf1[level, 0:OWN])
-        table = vm["gather1"][level, PAD : 2 * PAD, OWN : OWN + DIAG_AT]
-        rest.append(own + dot(table[:, LON_AT:DIAG_AT], buf1[level, OWN + LON_AT : OWN + DIAG_AT]))
+    near, nearer = OWN + LON_AT, OWN + LON_LAST
+    rest = [own[level] + dot(vm["lon1"][level], buf1[level, near:nearer]) for level in range(2)]
     fine(jnp.concatenate(rest, axis=0), [(0, 1), (1, 1)])
     for level in range(2):
         two[level].update(send(1, level, (3,), buf2, buf2, RESULTS))
@@ -323,6 +330,7 @@
     for level in range(2):
         two[level].update(send(1, level, (4,), buf2, buf2, RESULTS))
     for level in range(2):
+        one[level][3].wait_recv()
         one[level][2].wait_recv()
     last = [dot(vm["gather1"][level, 3 * PAD : 4 * PAD], buf1[level]) for level in range(2)]
     fine(jnp.concatenate(last, axis=0), [(0, 3), (1, 3)])
@@ -331,12 +339,15 @@
     for k in range(4):
         up_pad[:, k * 256 : k * 256 + C] = vm["up_weight"][:, k * C : (k + 1) * C]
     need("gather2", "send3", "merge_gain", "merge_weight", "coarse_gain", "coarse_qkv", "coarse_proj")
-    need("up_gain", "out_weight", "final")
-
-    for level in range(2):
-        for copy in two[level].values():
-            copy.wait_recv()
-    cells = [dot(vm["gather2"][...], buf2[level]) for level in range(2)]
+    need("up_gain", "out_weight", "final", "final_b", "gather2b")
+
+    for level in range(2):
+        for i in (0, 1, 2, 4):
+            two[level][i].wait_recv()
+    soon = [dot(vm["gather2"][...], buf2[level, 0:SOON]) for level in range(2)]
+    for level in range(2):
+        two[level][3].wait_recv()
+    cells = [soon[level] + dot(vm["gather2b"][...], buf2[level, SOON:]) for level in range(2)]
     group = [
         jnp.concatenate([cells[level][(k ^ m) * PAD : ((k ^ m) + 1) * PAD] for level, m in enumerate(MIRROR)], axis=0)
         for k in range(4)
@@ -378,13 +389,12 @@
         snd3[level] = dot(vm["send3"][PAD : 4 * PAD], mine).astype(BF)
         three.append(send(2, level, (0, 1, 2), snd3, buf3, ENCODED))
         mines.append(mine)
-    for level in range(2):
-        buf3[level, 0:PAD] = dot(vm["send3"][0:PAD], mines[level]).astype(BF)
-
+    mines = [dot(vm["send3"][0:PAD], mine).astype(BF) for mine in mines]
+    mines = [dot(vm["final"][level], mines[level]) for level in range(2)]
     for level in range(2):
         for copy in three[level].values():
             copy.wait_recv()
-        out_ref[level] = dot(vm["final"][level], buf3[level]).astype(BF)
+        out_ref[level] = (mines[level] + dot(vm["final_b"][level], buf3[level])).astype(BF)
     for copies in one + two + three:
         for copy in copies.values():
             copy.wait_send()
@@ -414,7 +424,7 @@
         pltpu.VMEM((2, 2, PAD, 6 * PAD), F32),
         pltpu.VMEM((2, OWN + HALO, C), BF),
         pltpu.VMEM((2, 4 * PAD + HALO2, C), BF),
-        pltpu.VMEM((2, 4 * PAD, C), BF),
+        pltpu.VMEM((2, 3 * PAD, C), BF),
         pltpu.VMEM((2, HALO, C), BF),
         pltpu.VMEM((2, 3 * PAD, C), BF),
         pltpu.SemaphoreType.DMA((len(args) - 1,)),

time: 31.4 us -> 31.3 us (level)
  no operation moved by 1% of the time
where the time goes in v7:
time: 31.3 us; the launch traced here: 31.1 us
  Pallas kernels  30.4 us (97%)
  local copies, waits for them, and re-layouts  0.72 us (2%)
    pallas_call x1, Pallas kernels, body(): pl.pallas_call(functools.partial(kernel, lat_n, lon_n), out_shape=jax.Sha...  30.4 us
    unnamed x1, local copies, waits for them, and re-layouts  0.72 us

profile of v7, /device:TPU:2, one launch (start us, length us, event | category | flops | bytes accessed | tf_op | source)
XLA Modules:
  0.0 31.1 jit_solution(13115461195267629737)
XLA Ops:
  0.0 30.4 %shard_map.217 = bf16[2,288,192]{2,1,0:T(8,128)(2,1)S(1)} custom-call(bf16[2,288,192]{2,1,0:T(8,128)(2,1)} %bitcast.3, f32[192]{0:T(256)} %refs_1_.1, bf16[192,576]{1,0:T(8,128)(2,1)} %refs_2_.1, bf16[192,192]{1,0:T(8,128)(2,1)} %refs_3_.1, f32[768]{0:T(1024)} %refs_4_.1, bf16[768,384]{1,0:T(8,128)(2,1)} %refs_5_.1, f32[384]{0:T(512)} %refs_6_.1, ...), custom_call_target="tpu_custom_call" | custom-call | tf_op jit(solution)/shard_map/pallas_call | solution.py:435
  30.4 0.7 %copy.25 = bf16[2,12,24,192]{3,2,1,0:T(8,128)(2,1)} copy(bf16[2,12,24,192]{3,2,1,0:T(8,128)(2,1)S(1)} %bitcast.2) | data formatting | bytes 442368

commit v8 on v7

--- a/solution.py
+++ b/solution.py
@@ -42,7 +42,7 @@
     (DIAG_AT, OWN + DIAG_AT, 32, 2),
     (LON_LAST, OWN + LON_LAST, 32, 1),
 )
-ENCODED = ((2 * PAD, 2 * PAD, PAD, 2), (PAD, PAD, PAD, 0), (0, 0, PAD, 1))
+ENCODED = ((PAD, PAD, PAD, 0), (2 * PAD, 2 * PAD, PAD, 2), (0, 0, PAD, 1))
 
 
 def one_hot(rows, cols, pairs):
@@ -244,7 +244,7 @@
             loads[n] = pltpu.make_async_copy(hbm[n], vm[n], load_sem.at[order.index(n)])
             loads[n].start()
 
-    load(*order[:len(EARLY)])
+    load(*order)
 
     def need(*wanted):
         for n in wanted:
@@ -278,7 +278,6 @@
     for i in (0, 1, 3, 2):
         for level in range(2):
             one[level].update(send(0, level, (i,), snd1, buf1, TOKENS))
-    load(*order[len(EARLY):])
 
     need("qkv_weight", "far")
     zero = jnp.zeros((C, 64), BF)

time: 31.3 us -> 30.9 us (0.987)
    pallas_call x1, Pallas kernels: 30.4 us -> 30.1 us  [body(): pl.pallas_call(functools.partial(kernel, lat_n, lon_n), out_shape=jax.Sha...]
where the time goes in v8:
time: 30.9 us; the launch traced here: 30.8 us
  Pallas kernels  30.1 us (97%)
  local copies, waits for them, and re-layouts  0.72 us (2%)
    pallas_call x1, Pallas kernels, body(): pl.pallas_call(functools.partial(kernel, lat_n, lon_n), out_shape=jax.Sha...  30.1 us
    unnamed x1, local copies, waits for them, and re-layouts  0.72 us

profile of v8, /device:TPU:2, one launch (start us, length us, event | category | flops | bytes accessed | tf_op | source)
XLA Modules:
  0.0 30.8 jit_solution(11014364144976543213)
XLA Ops:
  0.0 30.1 %shard_map.217 = bf16[2,288,192]{2,1,0:T(8,128)(2,1)S(1)} custom-call(bf16[2,288,192]{2,1,0:T(8,128)(2,1)} %bitcast.3, f32[192]{0:T(256)} %refs_1_.1, bf16[192,576]{1,0:T(8,128)(2,1)} %refs_2_.1, bf16[192,192]{1,0:T(8,128)(2,1)} %refs_3_.1, f32[768]{0:T(1024)} %refs_4_.1, bf16[768,384]{1,0:T(8,128)(2,1)} %refs_5_.1, f32[384]{0:T(512)} %refs_6_.1, ...), custom_call_target="tpu_custom_call" | custom-call | tf_op jit(solution)/shard_map/pallas_call | solution.py:434
  30.1 0.7 %copy.25 = bf16[2,12,24,192]{3,2,1,0:T(8,128)(2,1)} copy(bf16[2,12,24,192]{3,2,1,0:T(8,128)(2,1)S(1)} %bitcast.2) | data formatting | bytes 442368

commit v9 on v8

--- a/solution.py
+++ b/solution.py
@@ -275,7 +275,7 @@
         snd1[level] = dot(vm["send1"][level], buf1[level, 0:OWN]).astype(BF)
     pl.semaphore_wait(barrier, 8)
     one = [{}, {}]
-    for i in (0, 1, 3, 2):
+    for i in (0, 1, 2, 3):
         for level in range(2):
             one[level].update(send(0, level, (i,), snd1, buf1, TOKENS))
 

time: 30.9 us -> 30.9 us (level)
  no operation moved by 1% of the time
where the time goes in v9:
time: 30.9 us; the launch traced here: 30.8 us
  Pallas kernels  30.1 us (97%)
  local copies, waits for them, and re-layouts  0.72 us (2%)
    pallas_call x1, Pallas kernels, body(): pl.pallas_call(functools.partial(kernel, lat_n, lon_n), out_shape=jax.Sha...  30.1 us
    unnamed x1, local copies, waits for them, and re-layouts  0.72 us

profile of v9, /device:TPU:2, one launch (start us, length us, event | category | flops | bytes accessed | tf_op | source)
XLA Modules:
  0.0 30.8 jit_solution(17119533430134853411)
XLA Ops:
  0.0 30.1 %shard_map.217 = bf16[2,288,192]{2,1,0:T(8,128)(2,1)S(1)} custom-call(bf16[2,288,192]{2,1,0:T(8,128)(2,1)} %bitcast.3, f32[192]{0:T(256)} %refs_1_.1, bf16[192,576]{1,0:T(8,128)(2,1)} %refs_2_.1, bf16[192,192]{1,0:T(8,128)(2,1)} %refs_3_.1, f32[768]{0:T(1024)} %refs_4_.1, bf16[768,384]{1,0:T(8,128)(2,1)} %refs_5_.1, f32[384]{0:T(512)} %refs_6_.1, ...), custom_call_target="tpu_custom_call" | custom-call | tf_op jit(solution)/shard_map/pallas_call | solution.py:434
  30.1 0.7 %copy.25 = bf16[2,12,24,192]{3,2,1,0:T(8,128)(2,1)} copy(bf16[2,12,24,192]{3,2,1,0:T(8,128)(2,1)S(1)} %bitcast.2) | data formatting | bytes 442368
